TPU v7x, 256 devices: a whole 4x4x8 slice. The times are simulated.
256 devices in a mesh: group: 16 (over x_hi, z), fsdp: 16 (over y, x_lo, core).
Axes of the slice: x: 4 (x_hi: 2, x_lo: 2; x = x_hi * 2 + x_lo), y: 4, z: 8, core: 2. Of those that a mesh axis runs over, the one named last changes fastest.
Arguments:
- activations: bfloat16 [16, 4096, 8192], P('group', 'fsdp'), may hold values from -6 to 6
- targets: bfloat16 [16, 4096, 512], P('group', 'fsdp'), may hold values from -6 to 6
- token_ids: int32 [16, 4096], P('group', 'fsdp'), may hold values from 0 to 128255, as said below
- sync_fragment: int32 [4], replicated, may hold values from 0 to 3, each once
- params: float32 [16, 8192, 512], P('group', 'fsdp'), may hold values from -6 to 6
- adam_m: float32 [16, 8192, 512], P('group', 'fsdp'), may hold values from -0.0007324219 to 0.0007324219
- adam_v: float32 [16, 8192, 512], P('group', 'fsdp'), may hold values from 7.450581e-09 to 1.1920929e-07
- anchor: float32 [8192, 512], P('fsdp'), may hold values from -6 to 6
- momentum: float32 [8192, 512], P('fsdp'), may hold values from -4 to 4
Outputs:
- new_params: float32 [16, 8192, 512], P('group', 'fsdp')
- new_adam_m: float32 [16, 8192, 512], P('group', 'fsdp')
- new_adam_v: float32 [16, 8192, 512], P('group', 'fsdp')
- new_anchor: float32 [8192, 512], P('fsdp')
- new_momentum: float32 [8192, 512], P('fsdp')
Inputs may be any that keep to these rules, and one draw needn't show every extreme that they name: `token_ids`: 0 marks padding, other values are vocabulary ids; in each aligned block of 256 tokens the padding stands at the end and covers at most three quarters of the block. `sync_fragment`: each fragment appears once.
All inputs are finite; a program needn't handle non-finite values.
Results may differ from a plain program's by a relative error of at most 0.0028.
Values may be sent and summed in bfloat16 or wider, within the bound.
A program may use at most 128 MiB of HBM per device.

v0:
```python
import jax
import jax.numpy as jnp
from jax import lax
from jax.sharding import PartitionSpec as P

D = 8192
HEAD = 128


beta_one = 0.9
beta_two = 0.999
learn_rate = 0.05
decay_rate = 0.1
adam_epsilon = 1e-08
outer_rate = 0.7
outer_beta = 0.9
merge_weight = 0.5


def outer_update(anchor, momentum, weight, start):
    anchor_cols = lax.dynamic_slice_in_dim(anchor, start, HEAD, 1)
    worker_cols = lax.dynamic_slice_in_dim(weight, start, HEAD, 1)
    total = lax.psum(anchor_cols - worker_cols, "group")
    delta = total / lax.axis_size("group")
    moment_frag = outer_beta * lax.dynamic_slice_in_dim(momentum, start, HEAD, 1) + delta
    anchor_frag = anchor_cols - outer_rate * (delta + outer_beta * moment_frag)
    return (moment_frag, anchor_frag)


def on_device(
    activations, targets, token_ids, sync_fragment, params, adam_m, adam_v, anchor, momentum
):
    inputs = activations[0]
    target = targets[0].astype(jnp.float32)
    weight = params[0]
    scale = float(D) ** (-0.5)
    start = sync_fragment[0] * HEAD
    arrived = sync_fragment[1] * HEAD
    live = (token_ids[0] != 0).astype(jnp.float32)
    count = lax.psum(jnp.sum(live), "fsdp")
    weights = weight.astype(jnp.bfloat16)
    columns = inputs
    keys = (
        jnp.dot(
            columns,
            lax.all_gather(weights, "fsdp", axis=0, tiled=True),
            preferred_element_type=jnp.float32,
        )
        * scale
    )
    resid = (live[:, None] * (keys - target) / count).astype(jnp.bfloat16)
    columns = inputs
    grad = (
        lax.psum_scatter(
            jnp.einsum("tk,tc->kc", columns, resid, preferred_element_type=jnp.float32),
            "fsdp",
            scatter_dimension=0,
            tiled=True,
        )
        * scale
    )
    first = beta_one * adam_m[0] + (1.0 - beta_one) * grad
    second = beta_two * adam_v[0] + (1.0 - beta_two) * grad * grad
    stepped = weight - learn_rate * (
        first / (jnp.sqrt(second) + adam_epsilon) + decay_rate * weight
    )
    moment_frag, anchor_frag = outer_update(anchor, momentum, weight, start)
    arrived_cols = lax.dynamic_slice_in_dim(anchor, arrived, HEAD, 1)
    merged = (
        merge_weight * lax.dynamic_slice_in_dim(stepped, arrived, HEAD, 1)
        + (1.0 - merge_weight) * arrived_cols
    )
    new_params = lax.dynamic_update_slice_in_dim(stepped, merged, arrived, 1)
    new_anchor = lax.dynamic_update_slice_in_dim(anchor, anchor_frag, start, 1)
    new_momentum = lax.dynamic_update_slice_in_dim(momentum, moment_frag, start, 1)
    return (new_params[None], first[None], second[None], new_anchor, new_momentum)


def solution(mesh):
    placed = (
        P("group", "fsdp", None),
        P("group", "fsdp", None),
        P("group", "fsdp"),
        P(),
        P("group", "fsdp", None),
        P("group", "fsdp", None),
        P("group", "fsdp", None),
        P("fsdp", None),
        P("fsdp", None),
    )
    return jax.shard_map(
        on_device,
        mesh=mesh,
        in_specs=placed,
        out_specs=(
            P("group", "fsdp", None),
            P("group", "fsdp", None),
            P("group", "fsdp", None),
            P("fsdp", None),
            P("fsdp", None),
        ),
        check_vma=False,
    )
```

profile of v0, /device:TPU:160, one launch (start us, length us, event | category | flops | bytes accessed | tf_op | source)
XLA Modules:
  0.0 290.7 jit_solution(8383053424030759587)
XLA Ops:
  8.1 1.3 copy.28
  9.3 2.6 copy.29
  12.0 1.6 copy.14
  13.5 0.9 bitcast_convert_fusion
  14.4 0.0 all-reduce.2.cloned.1.call-start
  14.5 0.7 fusion.31
  15.8 1.7 bitcast_subtract_fusion.1
  17.6 0.6 fusion.30
  18.2 31.5 %psum.14 = f32[]{:T(128)} all-reduce(f32[]{:T(128)} %fusion.30), channel_id=1, replica_groups=mesh['group'=16,'fsdp'=16] {'fsdp'}, use_global_device_ids=true, to_apply=%region_1.0 | all-reduce | flops 1 | bytes 8 | tf_op jit(solution)/shard_map/psum | solution.py:40
  49.7 21.0 %all-gather.2.cloned.1.call-done = bf16[8192,512]{0,1:T(8,128)(2,1)} async-done(((bf16[512,512]{0,1:T(8,128)(2,1)}), bf16[8192,512]{0,1:T(8,128)(2,1)}) %all-gather.2.cloned.1.call-update) | async-done | bytes 8388624 | tf_op jit(solution)/shard_map/all_gather | solution.py:46
  70.7 16.9 %convolution_bitcast_fusion = f32[8192,512]{0,1:T(8,128)} fusion(bf16[1,256,8192]{2,1,0:T(8,128)(2,1)} %param.9, bf16[8192,512]{0,1:T(8,128)(2,1)} %all-gather.2.cloned.1.call-done, bf16[1,256,512]{2,1,0:T(8,128)(2,1)S(1)} %copy-done.3, f32[]{:T(128)} %psum.14, f32[256]{0:T(256)S(1)} %bitcast.61), kind=kOutput, calls=%fused_computation | convolution fusion | flops 4295753728 | bytes 29623300 | tf_op jit(solution)/shard_map/tk,tc->kc/dot_general | solution.py:55
  88.4 0.4 copy-done.1
  88.9 0.3 copy.16
  89.2 1.6 copy.15
  90.8 79.6 %all-reduce.2.cloned.1.call-done = f32[512,128]{1,0:T(8,128)} async-done(((f32[512,128]{1,0:T(8,128)}), f32[512,128]{1,0:T(8,128)}) %all-reduce.2.cloned.1.call-update) | async-done | bytes 262160 | tf_op jit(solution)/shard_map/psum | solution.py:23
  170.4 2.1 fusion.28
  172.4 0.8 copy.21
  173.3 100.2 %reduce-scatter.2.cloned.1.call-done = f32[512,512]{0,1:T(8,128)} async-done(((f32[8192,512]{0,1:T(8,128)}), f32[512,512]{0,1:T(8,128)}) %reduce-scatter.2.cloned.1.call-update) | async-done | bytes 1048592 | tf_op jit(solution)/shard_map/reduce_scatter | solution.py:54
  273.5 3.3 %fusion.27 = (f32[1,512,512]{1,2,0:T(8,128)}, f32[512,512]{0,1:T(8,128)S(1)}, f32[1,512,512]{1,2,0:T(8,128)}) fusion(f32[512,512]{0,1:T(8,128)} %reduce-scatter.2.cloned.1.call-done, f32[1,512,512]{1,2,0:T(8,128)S(1)} %copy.16, f32[1,512,512]{1,2,0:T(8,128)S(1)} %copy.15, f32[1,512,512]{1,2,0:T(8,128)S(1)} %copy.14), kind=kLoop, calls=%fused_computation.25 | loop fusion | flops 3670016 | bytes 7340032 | tf_op jit(solution)/shard_map/broadcast_in_dim | solution.py:76
  276.8 0.1 copy.25
  276.9 0.1 bitcast_dynamic-update-slice_fusion
  276.9 1.3 copy.18
  278.2 2.5 copy.19
  280.7 2.5 copy.20
  (17 shorter events, 0.2 us)
Async XLA Ops:
  8.0 62.7 %copy-start.3 = (bf16[1,256,512]{2,1,0:T(8,128)(2,1)S(1)}, bf16[1,256,512]{2,1,0:T(8,128)(2,1)}, u32[]{:S(2)}) copy-start(bf16[1,256,512]{2,1,0:T(8,128)(2,1)} %param.10) | copy-start | bytes 786436
  8.0 9.6 %copy-start.5 = (s32[1,256]{1,0:T(1,128)S(1)}, s32[1,256]{1,0:T(1,128)}, u32[]{:S(2)}) copy-start(s32[1,256]{1,0:T(1,128)} %param.11) | copy-start | bytes 3076
  8.0 6.5 %copy-start.4 = (s32[4]{0:T(128)S(1)}, s32[4]{0:T(128)}, u32[]{:S(2)}) copy-start(s32[4]{0:T(128)} %param.12) | copy-start | bytes 52
  8.0 62.7 %all-gather.2.cloned.1.call-start = ((), (), s32[]{:S(2)}) async-start(), calls=%async_computation.1 | async-start | bytes 8912896 | tf_op jit(solution)/shard_map/all_gather | solution.py:46
  9.3 78.3 %copy-start = (f32[512,512]{1,0:T(8,128)}, f32[512,512]{1,0:T(8,128)S(1)}, u32[]{:S(2)}) copy-start(f32[512,512]{1,0:T(8,128)S(1)} %copy.28) | copy-start | bytes 3145732
  14.4 155.9 %all-reduce.2.cloned.1.call-start = ((), (), s32[]{:S(2)}) async-start(), calls=%async_computation.3 | async-start | bytes 524288 | tf_op jit(solution)/shard_map/psum | solution.py:23
  17.5 256.0 %reduce-scatter.2.cloned.1.call-start = ((), (), s32[]{:S(2)}) async-start(), calls=%async_computation.2 | async-start | bytes 17825792 | tf_op jit(solution)/shard_map/reduce_scatter | solution.py:54
  87.6 1.2 copy-start.1
  173.3 103.6 %copy-start.2 = (f32[512,128]{0,1:T(8,128)S(1)}, f32[512,128]{0,1:T(8,128)}, u32[]{:S(2)}) copy-start(f32[512,128]{0,1:T(8,128)} %copy.21) | copy-start | bytes 786436
Sparse Core Ops, SparseCore 0:
  14.5 56.1 all-gather.1
  87.8 185.6 reduce-scatter.1
Sparse Core Ops, SparseCore 1:
  18.1 152.2 all-reduce.1
where the time goes:
time: 295 us; the launch traced here: 291 us
  waiting for transfers between devices  201 us (68%)
  blocking collectives  31.5 us (11%)
  between operations  17 us (6%)
  matrix products  16.9 us (6%)
  local copies, waits for them, and re-layouts  15.7 us (5%)
  other arithmetic  8.57 us (3%)
    reduce_scatter x1, waiting for transfers between devices, on_device(): lax.psum_scatter(jnp.einsum('tk,tc->kc', columns, resid, preferred_elemen...  100 us
    psum x1, waiting for transfers between devices, outer_update(): total = lax.psum(anchor_cols - worker_cols, 'group')  79.6 us
    psum x1, blocking collectives, on_device(): count = lax.psum(jnp.sum(live), 'fsdp')  31.5 us
    all_gather x1, waiting for transfers between devices, on_device(): lax.all_gather(weights, 'fsdp', axis=0, tiled=True)  21 us
    dot_general x1, matrix products, on_device(): jnp.einsum('tk,tc->kc', columns, resid, preferred_element_type=jnp.float32)  16.9 us
    unnamed x22, local copies, waits for them, and re-layouts  15.1 us
  transfers between devices with their start and end apart: 3, of which 3 were waited for; matrix products, arithmetic and copies ran while one was open for 8% of the time, Pallas kernels for 0%

commit v1 on v0

v1 whole, which is shorter than its diff:
```python
import functools

import jax
import jax.numpy as jnp
from jax import lax
from jax.experimental import pallas as pl
from jax.experimental.pallas import tpu as pltpu
from jax.sharding import PartitionSpec as P

HEAD = 128
MESH = pl.DeviceIdType.MESH
F32 = jnp.float32
BF16 = jnp.bfloat16

beta_one = 0.9
beta_two = 0.999
learn_rate = 0.05
decay_rate = 0.1
adam_epsilon = 1e-08
outer_rate = 0.7
outer_beta = 0.9
merge_weight = 0.5

NF = 16
NZ = 8

(S_OWN, YP_OWN, YM_OWN, X_OWN, YP_F, YM_F, YP_X, YM_X, X_FA, X_FB,
 S_YP, S_YM, S_X, S_YA, S_YB, S_YPX, S_YMX, S_XA, S_XB) = range(19)
GS = 19
X1, Y1P, Y1M, Y2P, Y2M, Y3PB, Y3PA, Y3MA, Y3MB, X2 = range(27, 37)
KINDS = 37


def sync_kernel(scale, act, tgt, ids, frag, params, anchor, grad_out, delta_out,
                xv, xt, tv, pv, av, live, total, wg, gown, gsend, gsib,
                rx1, ry1p, ry1m, ry2p, ry2m, ry3p, ry3m, rx2,
                tx1, ty1p, ty1m, ty2p, ty2m, ty3p, ty3m, tx2,
                gout, dd, zrecv, zs, xrecv, dall, cs, cr,
                ssem, rsem, zsem, zrsem, csem, crsem, lsem):
    nq, _, rows, cw = wg.shape
    tokens = xv.shape[0]
    half = rows // 2
    g, me = lax.axis_index("group"), lax.axis_index("fsdp")
    y, x, c = me // 4, lax.rem(me // 2, 2), lax.rem(me, 2)
    z, far = lax.rem(g, NZ), g // NZ
    yp, ym, y2, xo, co = lax.rem(y + 1, 4), lax.rem(y + 3, 4), lax.rem(y + 2, 4), 1 - x, 1 - c
    groups = lax.axis_size("group")

    def at(yy, xx, cc):
        return yy * 4 + xx * 2 + cc

    def zdev(k):
        return (far * NZ + lax.rem(z + k, NZ), me)

    sib, up, down, side = ((g, at(y, x, co)), (g, at(yp, x, c)), (g, at(ym, x, c)), (g, at(y, xo, c)))
    across = ((1 - far) * NZ + z, me)

    def load(src, dst, k):
        return pltpu.make_async_copy(src, dst, lsem.at[k])

    l_params = load(params.at[0], pv, 0)
    l_params.start()
    l_anchor = load(anchor, av, 1)
    l_anchor.start()
    l_act = load(act.at[0], xv, 2)
    l_act.start()
    l_tgt = load(tgt.at[0], tv, 3)
    l_tgt.start()

    row = jnp.where(ids[...] != 0, 1.0, 0.0).astype(F32)
    live[...] = jnp.transpose(jnp.broadcast_to(row, (HEAD, tokens)))
    cs[0] = jnp.broadcast_to(jnp.sum(row), cs.shape[1:])

    peers = [sib, up, down, side]
    if groups > 1:
        peers += [zdev(k) for k in range(1, NZ)] + [across]
    barrier = pltpu.get_barrier_semaphore()
    for peer in peers:
        pl.semaphore_signal(barrier, inc=1, device_id=peer, device_id_type=MESH)
    l_params.wait()
    for q in range(nq):
        wg[q, me] = pv[:, q * cw:(q + 1) * cw].astype(BF16)
    pl.semaphore_wait(barrier, len(peers))

    sends = []

    def remote(src, dst, q, kind, peer):
        return pltpu.make_async_remote_copy(
            src_ref=src, dst_ref=dst, send_sem=ssem.at[q, kind], recv_sem=rsem.at[q, kind],
            device_id=peer, device_id_type=MESH)

    def send(src, dst, q, kind, peer):
        copy = remote(src, dst, q, kind, peer)
        copy.start()
        sends.append(copy)

    def arrived(dst, q, kind):
        remote(dst, dst, q, kind, sib).wait_recv()

    def part(name):
        return {"a": pl.ds(0, half), "b": pl.ds(half, half), None: pl.ds(0, rows)}[name]

    def gsend_w(q, kind, peer, shard, rng=None):
        ref = wg.at[q, shard, part(rng)]
        send(ref, ref, q, kind, peer)

    def got_w(q, kind, shard, rng=None):
        arrived(wg.at[q, shard, part(rng)], q, kind)

    y1, y3 = y + 1 - 2 * lax.rem(y, 2), 3 - y
    count_peers = [sib, side, (g, at(y1, x, c)), (g, at(y3, x, c))]

    def count_send(k):
        copy = pltpu.make_async_remote_copy(
            src_ref=cs.at[k], dst_ref=cr.at[k], send_sem=csem.at[k], recv_sem=crsem.at[k],
            device_id=count_peers[k], device_id_type=MESH)
        copy.start()
        sends.append(copy)

    def count_step(k):
        pltpu.make_async_remote_copy(
            src_ref=cs.at[k], dst_ref=cr.at[k], send_sem=csem.at[k], recv_sem=crsem.at[k],
            device_id=count_peers[k], device_id_type=MESH).wait_recv()
        s = cs[k] + cr[k]
        if k < 3:
            cs[k + 1] = s
            count_send(k + 1)
        else:
            total[...] = s

    def zcopy(src, dst, k, peer):
        return pltpu.make_async_remote_copy(
            src_ref=src, dst_ref=dst, send_sem=zsem.at[k], recv_sem=zrsem.at[k],
            device_id=peer, device_id_type=MESH)

    def delta_start():
        l_anchor.wait()
        diff = av[:, :cw] - pv[:, :cw]
        for f in range(1, nq):
            cols = slice(f * cw, (f + 1) * cw)
            diff = jnp.where(jnp.full(diff.shape, frag[0]) == f, av[:, cols] - pv[:, cols], diff)
        dd[...] = diff.reshape(dd.shape)
        if groups > 1:
            for k in range(1, NZ):
                copy = zcopy(dd.at[lax.rem(z + k, NZ)], zrecv.at[k - 1], k - 1, zdev(k))
                copy.start()
                sends.append(copy)

    def delta_sum():
        if groups > 1:
            s = dd[z]
            for k in range(1, NZ):
                zcopy(zrecv.at[k - 1], zrecv.at[k - 1], k - 1, zdev(k)).wait_recv()
            for k in range(1, NZ):
                s = s + zrecv[k - 1]
            zs[...] = s
            copy = zcopy(zs, xrecv, NZ - 1, across)
            copy.start()
            sends.append(copy)

    def delta_share():
        if groups > 1:
            zcopy(zs, xrecv, NZ - 1, across).wait_recv()
            dall[z] = (zs[...] + xrecv[...]) / groups
            for k in range(1, NZ):
                copy = zcopy(dall.at[z], dall.at[z], NZ + k - 1, zdev(k))
                copy.start()
                sends.append(copy)
        else:
            dall[...] = dd[...]

    def delta_end():
        if groups > 1:
            for k in range(1, NZ):
                slot = dall.at[lax.rem(z + NZ - k, NZ)]
                zcopy(slot, slot, NZ + k - 1, zdev(k)).wait_recv()
        load(dall, delta_out, 4).start()

    def gather_own(q):
        own = at(y, x, c)
        gsend_w(q, YP_OWN, up, own)
        gsend_w(q, YM_OWN, down, own)
        gsend_w(q, X_OWN, side, own)
        gsend_w(q, S_OWN, sib, own)

    def gather_one(q):
        got_w(q, X_OWN, at(y, xo, c))
        gsend_w(q, YP_X, up, at(y, xo, c))
        gsend_w(q, YM_X, down, at(y, xo, c))
        gsend_w(q, S_X, sib, at(y, xo, c))
        got_w(q, YP_OWN, at(ym, x, c))
        gsend_w(q, YP_F, up, at(ym, x, c), "a")
        gsend_w(q, S_YP, sib, at(ym, x, c))
        got_w(q, YM_OWN, at(yp, x, c))
        gsend_w(q, YM_F, down, at(yp, x, c), "b")
        gsend_w(q, S_YM, sib, at(yp, x, c))

    def gather_two(q):
        got_w(q, YP_F, at(y2, x, c), "a")
        gsend_w(q, X_FA, side, at(y2, x, c), "a")
        gsend_w(q, S_YA, sib, at(y2, x, c), "a")
        got_w(q, YM_F, at(y2, x, c), "b")
        gsend_w(q, X_FB, side, at(y2, x, c), "b")
        gsend_w(q, S_YB, sib, at(y2, x, c), "b")

    def gather_three(q):
        got_w(q, YP_X, at(ym, xo, c))
        gsend_w(q, S_YPX, sib, at(ym, xo, c))
        got_w(q, YM_X, at(yp, xo, c))
        gsend_w(q, S_YMX, sib, at(yp, xo, c))
        got_w(q, X_FA, at(y2, xo, c), "a")
        gsend_w(q, S_XA, sib, at(y2, xo, c), "a")
        got_w(q, X_FB, at(y2, xo, c), "b")
        gsend_w(q, S_XB, sib, at(y2, xo, c), "b")

    def gather_end(q):
        got_w(q, S_OWN, at(y, x, co))
        got_w(q, S_X, at(y, xo, co))
        got_w(q, S_YP, at(ym, x, co))
        got_w(q, S_YM, at(yp, x, co))
        got_w(q, S_YA, at(y2, x, co), "a")
        got_w(q, S_YB, at(y2, x, co), "b")
        got_w(q, S_YPX, at(ym, xo, co))
        got_w(q, S_YMX, at(yp, xo, co))
        got_w(q, S_XA, at(y2, xo, co), "a")
        got_w(q, S_XB, at(y2, xo, co), "b")

    order = [(y2, xo), (yp, xo), (ym, xo), (y2, x), (yp, x), (ym, x), (y, xo), (y, x)]

    def compute(q):
        def body(i, acc):
            cols = pl.ds(pl.multiple_of(i * rows, rows), rows)
            return acc + jnp.dot(xv[:, cols], wg[q, i], preferred_element_type=F32)

        keys = lax.fori_loop(0, NF, body, jnp.zeros((tokens, cw), F32)) * scale
        target = tv[:, q * cw:(q + 1) * cw].astype(F32)
        resid = (live[...] * (keys - target) / total[0:1, 0:1]).astype(BF16)
        for j, (yy, xx) in enumerate(order):
            gsend[q, j] = jnp.dot(xt[at(yy, xx, co)], resid, preferred_element_type=F32).astype(BF16)
            send(gsend.at[q, j], gsib.at[q, j], q, GS + j, sib)
        for j, (yy, xx) in enumerate(order):
            gown[q, j] = jnp.dot(xt[at(yy, xx, c)], resid, preferred_element_type=F32)

    lo, hi = slice(0, half), slice(half, rows)

    def got_s(q, j):
        arrived(gsib.at[q, j], q, GS + j)

    def pair(q, j, rng=slice(None)):
        return gown[q, j, rng] + gsib[q, j, rng].astype(F32)

    def scatter_one(q):
        for j, buf, dst, kind, peer in ((0, tx1, rx1, X1, side), (1, ty1p, ry1p, Y1P, up), (2, ty1m, ry1m, Y1M, down)):
            got_s(q, j)
            buf[q] = pair(q, j).astype(BF16)
            send(buf.at[q], dst.at[q], q, kind, peer)
        got_s(q, 3)
        got_s(q, 4)
        ty3p[q, hi] = pair(q, 4, hi).astype(BF16)
        send(ty3p.at[q, part("b")], ry3p.at[q, part("b")], q, Y3PB, up)
        got_s(q, 5)
        ty3m[q, lo] = pair(q, 5, lo).astype(BF16)
        send(ty3m.at[q, part("a")], ry3m.at[q, part("a")], q, Y3MA, down)
        got_s(q, 6)
        got_s(q, 7)

    def scatter_two(q):
        arrived(rx1.at[q], q, X1)
        ty2p[q] = (pair(q, 3, lo) + rx1[q, lo].astype(F32)).astype(BF16)
        send(ty2p.at[q], ry2p.at[q], q, Y2P, up)
        ty2m[q] = (pair(q, 3, hi) + rx1[q, hi].astype(F32)).astype(BF16)
        send(ty2m.at[q], ry2m.at[q], q, Y2M, down)
        arrived(ry1p.at[q], q, Y1P)
        arrived(ry1m.at[q], q, Y1M)
        tx2[q] = (pair(q, 6) + ry1p[q].astype(F32) + ry1m[q].astype(F32)).astype(BF16)
        send(tx2.at[q], rx2.at[q], q, X2, side)

    def scatter_three(q):
        arrived(ry2p.at[q], q, Y2P)
        ty3p[q, lo] = (pair(q, 4, lo) + ry2p[q].astype(F32)).astype(BF16)
        send(ty3p.at[q, part("a")], ry3p.at[q, part("a")], q, Y3PA, up)
        arrived(ry2m.at[q], q, Y2M)
        ty3m[q, hi] = (pair(q, 5, hi) + ry2m[q].astype(F32)).astype(BF16)
        send(ty3m.at[q, part("b")], ry3m.at[q, part("b")], q, Y3MB, down)

    def out_copy(q):
        cols = pl.ds(q * cw, cw)
        return pltpu.make_async_copy(gout.at[:, cols], grad_out.at[:, cols], lsem.at[5 + q])

    def scatter_end(q):
        arrived(rx2.at[q], q, X2)
        arrived(ry3p.at[q, part("b")], q, Y3PB)
        arrived(ry3m.at[q, part("a")], q, Y3MA)
        arrived(ry3p.at[q, part("a")], q, Y3PA)
        arrived(ry3m.at[q, part("b")], q, Y3MB)
        s = pair(q, 7) + rx2[q].astype(F32) + ry3p[q].astype(F32) + ry3m[q].astype(F32)
        gout[:, q * cw:(q + 1) * cw] = s * scale
        out_copy(q).start()

    count_send(0)
    gather_own(0)
    gather_own(1)
    count_step(0)
    delta_start()
    l_act.wait()

    def turn(i):
        cols = pl.ds(pl.multiple_of(i * rows, rows), rows)
        xt[i] = jnp.transpose(xv[:, cols])

    def turn_some(first, last):
        def body(i, carry):
            turn(i)
            return carry
        lax.fori_loop(first, last, body, 0)

    turn_some(0, 4)
    count_step(1)
    gather_one(0)
    gather_own(2)
    turn_some(4, 8)
    count_step(2)
    gather_one(1)
    gather_own(3)
    turn_some(8, 12)
    gather_two(0)
    gather_one(2)
    turn_some(12, 16)
    gather_three(0)
    gather_two(1)
    gather_one(3)
    count_step(3)
    delta_sum()
    l_tgt.wait()
    gather_end(0)
    compute(0)
    gather_three(1)
    gather_two(2)
    scatter_one(0)
    gather_end(1)
    compute(1)
    gather_three(2)
    gather_two(3)
    scatter_two(0)
    scatter_one(1)
    delta_share()
    gather_end(2)
    compute(2)
    gather_three(3)
    scatter_three(0)
    scatter_two(1)
    scatter_one(2)
    gather_end(3)
    compute(3)
    scatter_three(1)
    scatter_two(2)
    scatter_one(3)
    scatter_end(0)
    scatter_three(2)
    scatter_two(3)
    scatter_end(1)
    delta_end()
    scatter_three(3)
    scatter_end(2)
    scatter_end(3)
    for copy in sends:
        copy.wait_send()
    load(dall, delta_out, 4).wait()
    for q in range(nq):
        out_copy(q).wait()


def sync(activations, targets, token_ids, sync_fragment, params, anchor):
    tokens, width = activations.shape[1:]
    rows, kv = params.shape[1:]
    nq = kv // HEAD
    piece = (nq, rows, HEAD)
    part = (nq, rows // 2, HEAD)
    anywhere = pl.BlockSpec(memory_space=pl.ANY)
    return pl.pallas_call(
        functools.partial(sync_kernel, float(width) ** (-0.5)),
        out_shape=(jax.ShapeDtypeStruct((rows, kv), F32), jax.ShapeDtypeStruct((NZ, rows // NZ, HEAD), F32)),
        in_specs=[anywhere, anywhere, pl.BlockSpec(memory_space=pltpu.VMEM), pl.BlockSpec(memory_space=pltpu.SMEM), anywhere, anywhere],
        out_specs=(anywhere, anywhere),
        scratch_shapes=[
            pltpu.VMEM((tokens, width), BF16),
            pltpu.VMEM((NF, rows, tokens), BF16),
            pltpu.VMEM((tokens, kv), BF16),
            pltpu.VMEM((rows, kv), F32),
            pltpu.VMEM((rows, kv), F32),
            pltpu.VMEM((tokens, HEAD), F32),
            pltpu.VMEM((8, HEAD), F32),
            pltpu.VMEM((nq, NF, rows, HEAD), BF16),
            pltpu.VMEM((nq, 8, rows, HEAD), F32),
            pltpu.VMEM((nq, 8, rows, HEAD), BF16),
            pltpu.VMEM((nq, 8, rows, HEAD), BF16),
            pltpu.VMEM(piece, BF16), pltpu.VMEM(piece, BF16), pltpu.VMEM(piece, BF16),
            pltpu.VMEM(part, BF16), pltpu.VMEM(part, BF16),
            pltpu.VMEM(piece, BF16), pltpu.VMEM(piece, BF16), pltpu.VMEM(piece, BF16),
            pltpu.VMEM(piece, BF16), pltpu.VMEM(piece, BF16), pltpu.VMEM(piece, BF16),
            pltpu.VMEM(part, BF16), pltpu.VMEM(part, BF16),
            pltpu.VMEM(piece, BF16), pltpu.VMEM(piece, BF16), pltpu.VMEM(piece, BF16),
            pltpu.VMEM((rows, kv), F32),
            pltpu.VMEM((NZ, rows // NZ, HEAD), F32),
            pltpu.VMEM((NZ - 1, rows // NZ, HEAD), F32),
            pltpu.VMEM((rows // NZ, HEAD), F32),
            pltpu.VMEM((rows // NZ, HEAD), F32),
            pltpu.VMEM((NZ, rows // NZ, HEAD), F32),
            pltpu.VMEM((4, 8, HEAD), F32),
            pltpu.VMEM((4, 8, HEAD), F32),
            pltpu.SemaphoreType.DMA((nq, KINDS)),
            pltpu.SemaphoreType.DMA((nq, KINDS)),
            pltpu.SemaphoreType.DMA((2 * NZ,)),
            pltpu.SemaphoreType.DMA((2 * NZ,)),
            pltpu.SemaphoreType.DMA((4,)),
            pltpu.SemaphoreType.DMA((4,)),
            pltpu.SemaphoreType.DMA((5 + nq,)),
        ],
        compiler_params=pltpu.CompilerParams(
            collective_id=0, has_side_effects=True, vmem_limit_bytes=54 * 2**20
        ),
        cost_estimate=pl.CostEstimate(
            flops=4 * tokens * width * kv, bytes_accessed=2 * tokens * width + 12 * rows * kv, transcendentals=0
        ),
        name="sync",
    )(activations, targets, token_ids, sync_fragment, params, anchor)


def update_kernel(frag, grad, delta, params, adam_m, adam_v, anchor, momentum,
                  new_params, new_m, new_v, new_anchor, new_momentum):
    fragment = pl.ds(pl.multiple_of(frag[0] * HEAD, HEAD), HEAD)
    arriving = pl.ds(pl.multiple_of(frag[1] * HEAD, HEAD), HEAD)
    slope = grad[...]
    weight = params[...]
    first = beta_one * adam_m[...] + (1.0 - beta_one) * slope
    second = beta_two * adam_v[...] + (1.0 - beta_two) * slope * slope
    new_m[...] = first
    new_v[...] = second
    new_params[...] = weight - learn_rate * (first / (jnp.sqrt(second) + adam_epsilon) + decay_rate * weight)
    new_params[:, arriving] = merge_weight * new_params[:, arriving] + (1.0 - merge_weight) * anchor[:, arriving]
    new_anchor[...] = anchor[...]
    new_momentum[...] = momentum[...]
    change = delta[...]
    moment = outer_beta * momentum[:, fragment] + change
    new_momentum[:, fragment] = moment
    new_anchor[:, fragment] = anchor[:, fragment] - outer_rate * (change + outer_beta * moment)


def update(frag, grad, delta, params, adam_m, adam_v, anchor, momentum, steps=4):
    rows, kv = grad.shape
    size = rows // steps
    worker = pl.BlockSpec((None, size, kv), lambda i: (0, i, 0))
    shared = pl.BlockSpec((size, kv), lambda i: (i, 0))
    strip = pl.BlockSpec((size, HEAD), lambda i: (i, 0))
    return pl.pallas_call(
        update_kernel,
        grid=(steps,),
        out_shape=[jax.ShapeDtypeStruct((1, rows, kv), F32)] * 3 + [jax.ShapeDtypeStruct((rows, kv), F32)] * 2,
        in_specs=[pl.BlockSpec(memory_space=pltpu.SMEM), shared, strip, worker, worker, worker, shared, shared],
        out_specs=[worker, worker, worker, shared, shared],
        name="update",
    )(frag, grad, delta, params, adam_m, adam_v, anchor, momentum)


def on_device(activations, targets, token_ids, sync_fragment, params, adam_m, adam_v, anchor, momentum):
    grad, delta = sync(activations, targets, token_ids, sync_fragment, params, anchor)
    delta = delta.reshape(delta.shape[0] * delta.shape[1], delta.shape[2])
    return tuple(update(sync_fragment, grad, delta, params, adam_m, adam_v, anchor, momentum))


def solution(mesh):
    worker = P("group", "fsdp", None)
    shared = P("fsdp", None)
    return jax.shard_map(
        on_device,
        mesh=mesh,
        in_specs=(worker, worker, P("group", "fsdp"), P(), worker, worker, worker, shared, shared),
        out_specs=(worker, worker, worker, shared, shared),
        check_vma=False,
    )
```

time: 295 us -> 89.6 us (0.30)
  the two profiles are of different devices: /device:TPU:160 before, /device:TPU:6 now
where the time goes in v1:
time: 89.6 us; the launch traced here: 89.5 us
  Pallas kernels  88.8 us (99%)
    pallas_call x1, Pallas kernels, sync(): pl.pallas_call(functools.partial(sync_kernel, float(width) ** (-0.5)), ou...  83.4 us
    pallas_call x1, Pallas kernels, update(): pl.pallas_call(update_kernel, grid=(steps,), out_shape=[jax.ShapeDtypeStr...  5.43 us

profile of v1, /device:TPU:6, one launch (start us, length us, event | category | flops | bytes accessed | tf_op | source)
XLA Modules:
  0.0 89.5 jit_solution(4058431177616698328)
XLA Ops:
  0.6 83.4 %sync.1 = (f32[512,512]{1,0:T(8,128)}, f32[8,64,128]{2,1,0:T(8,128)}) custom-call(bf16[1,256,8192]{2,1,0:T(8,128)(2,1)} %act.1, bf16[1,256,512]{2,1,0:T(8,128)(2,1)} %tgt.1, s32[1,256]{1,0:T(1,128)} %ids.1, s32[4]{0:T(128)} %frag.3, f32[1,512,512]{2,1,0:T(8,128)} %params.3, f32[512,512]{1,0:T(8,128)} %anchor.3), custom_call_target="tpu_custom_call" | custom-call | flops 4294967296 | bytes 7340032 | tf_op jit(solution)/shard_map/sync/pallas_call | solution.py:380
  84.0 5.4 %update.1 = (f32[1,512,512]{2,1,0:T(8,128)}, f32[1,512,512]{2,1,0:T(8,128)}, f32[1,512,512]{2,1,0:T(8,128)}, f32[512,512]{1,0:T(8,128)}, f32[512,512]{1,0:T(8,128)}) custom-call(s32[4]{0:T(128)} %frag.3, f32[512,512]{1,0:T(8,128)} %get-tuple-element.7.grad, f32[512,128]{1,0:T(8,128)} %bitcast.1, f32[1,512,512]{2,1,0:T(8,128)} %params.3, ...), custom_call_target="tpu_custom_call" | custom-call | tf_op jit(solution)/shard_map/update/pallas_call | solution.py:455

commit v2 on v0

v2 whole, which is shorter than its diff:
```python
import functools

import jax
import jax.numpy as jnp
from jax import lax
from jax.experimental import pallas as pl
from jax.experimental.pallas import tpu as pltpu
from jax.sharding import PartitionSpec as P

HEAD = 128
MESH = pl.DeviceIdType.MESH
F32 = jnp.float32
BF16 = jnp.bfloat16

beta_one = 0.9
beta_two = 0.999
learn_rate = 0.05
decay_rate = 0.1
adam_epsilon = 1e-08
outer_rate = 0.7
outer_beta = 0.9
merge_weight = 0.5

NF = 16
NZ = 8

EDGE = 80

(S_OWN, YP_OWN, YM_OWN, X_OWN, YP_F, YM_F, YP_X, YM_X, X_FA, X_FB, X_P, X_M,
 S_YP, S_YM, S_X, S_YA, S_YB, S_YPX, S_YMX, S_XA, S_XB) = range(21)
GS = 21
X1, Y1P, Y1M, XEP, XEM, Y2P, Y2M, Y3PB, Y3PA, Y3MA, Y3MB, X2 = range(29, 41)
KINDS = 41


def sync_kernel(scale, act, tgt, ids, fragments, params, anchor, grad_out, delta_out,
                frag, xv, xt, tv, pv, av, iv, live, total, wg, acc, gown, gsend, gsib,
                rx1, ry1p, ry1m, rxep, rxem, ry2p, ry2m, ry3p, ry3m, rx2,
                tx1, ty1p, ty1m, ty2p, ty2m, ty3p, ty3m, tx2,
                dd, zrecv, zs, xrecv, cs, cr,
                ssem, rsem, zsem, zrsem, csem, crsem, lsem):
    nq, _, rows, cw = wg.shape
    tokens = xv.shape[0]
    half = rows // 2
    edge = rxep.shape[1]
    g, me = lax.axis_index("group"), lax.axis_index("fsdp")
    y, x, c = me // 4, lax.rem(me // 2, 2), lax.rem(me, 2)
    z, far = lax.rem(g, NZ), g // NZ
    yp, ym, y2, xo, co = lax.rem(y + 1, 4), lax.rem(y + 3, 4), lax.rem(y + 2, 4), 1 - x, 1 - c
    groups = lax.axis_size("group")

    def at(yy, xx, cc):
        return yy * 4 + xx * 2 + cc

    def zdev(k):
        return (far * NZ + lax.rem(z + k, NZ), me)

    sib, up, down, side = ((g, at(y, x, co)), (g, at(yp, x, c)), (g, at(ym, x, c)), (g, at(y, xo, c)))
    across = ((1 - far) * NZ + z, me)

    peers = [sib, up, down, side]
    if groups > 1:
        peers += [zdev(k) for k in range(1, NZ)] + [across]
    barrier = pltpu.get_barrier_semaphore()
    for peer in peers:
        pl.semaphore_signal(barrier, inc=1, device_id=peer, device_id_type=MESH)

    def columns(q):
        return slice(q * cw, (q + 1) * cw)

    def load(src, dst, k):
        copy = pltpu.make_async_copy(src, dst, lsem.at[k])
        copy.start()
        return copy

    l_params = [load(params.at[0, :, columns(q)], pv.at[:, columns(q)], q) for q in range(nq)]
    l_ids = load(ids, iv, nq)
    l_act = load(act.at[0], xv, nq + 1)
    l_tgt = load(tgt.at[0], tv, nq + 2)
    l_anchor = load(anchor, av, nq + 3)
    l_frag = load(fragments, frag, nq + 4)

    sends = {}

    def start(copy, tag=None):
        copy.start()
        sends.setdefault(tag, []).append(copy)

    def settle(tag):
        for copy in sends.pop(tag, []):
            copy.wait_send()

    def settle_gather():
        for q in range(nq):
            settle(-1 - q)

    def remote(src, dst, q, kind, peer):
        return pltpu.make_async_remote_copy(
            src_ref=src, dst_ref=dst, send_sem=ssem.at[q, kind], recv_sem=rsem.at[q, kind],
            device_id=peer, device_id_type=MESH)

    def send(src, dst, q, kind, peer):
        start(remote(src, dst, q, kind, peer), q if kind >= GS else -1 - q)

    def arrived(dst, q, kind):
        remote(dst, dst, q, kind, sib).wait_recv()

    y1, y3 = y + 1 - 2 * lax.rem(y, 2), 3 - y
    count_peers = [sib, side, (g, at(y1, x, c)), (g, at(y3, x, c))]

    def count_copy(k):
        return pltpu.make_async_remote_copy(
            src_ref=cs.at[k], dst_ref=cr.at[k], send_sem=csem.at[k], recv_sem=crsem.at[k],
            device_id=count_peers[k], device_id_type=MESH)

    def count(k):
        if k == 0:
            l_ids.wait()
            row = jnp.where(iv[...] != 0, 1.0, 0.0).astype(F32)
            live[...] = jnp.transpose(jnp.broadcast_to(row, (HEAD, tokens)))
            part = jnp.broadcast_to(jnp.sum(row), cs.shape[1:])
        else:
            count_copy(k - 1).wait_recv()
            part = cs[k - 1] + cr[k - 1]
        if k < 4:
            cs[k] = part
            start(count_copy(k))
        else:
            total[...] = part

    def zcopy(src, dst, k, peer):
        return pltpu.make_async_remote_copy(
            src_ref=src, dst_ref=dst, send_sem=zsem.at[k], recv_sem=zrsem.at[k],
            device_id=peer, device_id_type=MESH)

    def mean_start():
        l_anchor.wait()
        l_frag.wait()
        diff = av[:, columns(0)] - pv[:, columns(0)]
        for f in range(1, nq):
            diff = jnp.where(jnp.full(diff.shape, frag[0]) == f, av[:, columns(f)] - pv[:, columns(f)], diff)
        dd[...] = diff.reshape(dd.shape)
        if groups > 1:
            for k in range(1, NZ):
                start(zcopy(dd.at[lax.rem(z + k, NZ)], zrecv.at[k - 1], k - 1, zdev(k)))

    def mean_sum():
        if groups > 1:
            for k in range(1, NZ):
                zcopy(zrecv.at[k - 1], zrecv.at[k - 1], k - 1, zdev(k)).wait_recv()
            s = dd[z]
            for k in range(1, NZ):
                s = s + zrecv[k - 1]
            zs[...] = s
            start(zcopy(zs, xrecv, NZ - 1, across))

    def mean_share():
        if groups > 1:
            zcopy(zs, xrecv, NZ - 1, across).wait_recv()
            delta_out[z] = (zs[...] + xrecv[...]) / groups
            for k in range(1, NZ):
                start(zcopy(delta_out.at[z], delta_out.at[z], NZ + k - 1, zdev(k)))
        else:
            delta_out[...] = dd[...]

    def mean_end():
        if groups > 1:
            for k in range(1, NZ):
                slot = delta_out.at[lax.rem(z + NZ - k, NZ)]
                zcopy(slot, slot, NZ + k - 1, zdev(k)).wait_recv()

    every, lo, hi = pl.ds(0, rows), pl.ds(0, half), pl.ds(half, half)
    first, but_first = pl.ds(0, edge), pl.ds(edge, rows - edge)
    last, but_last = pl.ds(rows - edge, edge), pl.ds(0, rows - edge)

    def give(q, kind, peer, shard, rng=every):
        ref = wg.at[q, shard, rng]
        send(ref, ref, q, kind, peer)

    def got(q, kind, shard, rng=every):
        arrived(wg.at[q, shard, rng], q, kind)

    def own(q):
        l_params[q].wait()
        wg[q, me] = pv[:, columns(q)].astype(BF16)
        give(q, X_OWN, side, me)
        give(q, YP_OWN, up, me)
        give(q, YM_OWN, down, me)
        give(q, S_OWN, sib, me)

    def from_side(q):
        shard = at(y, xo, c)
        got(q, X_OWN, shard)
        give(q, YP_X, up, shard, but_first)
        give(q, YM_X, down, shard, but_last)
        give(q, S_X, sib, shard)

    def from_down(q):
        shard = at(ym, x, c)
        got(q, YP_OWN, shard)
        give(q, YP_F, up, shard, lo)
        give(q, X_P, side, shard, first)
        give(q, S_YP, sib, shard)

    def from_up(q):
        shard = at(yp, x, c)
        got(q, YM_OWN, shard)
        give(q, YM_F, down, shard, hi)
        give(q, X_M, side, shard, last)
        give(q, S_YM, sib, shard)

    def far_lo(q):
        shard = at(y2, x, c)
        got(q, YP_F, shard, lo)
        give(q, X_FA, side, shard, lo)
        give(q, S_YA, sib, shard, lo)

    def far_hi(q):
        shard = at(y2, x, c)
        got(q, YM_F, shard, hi)
        give(q, X_FB, side, shard, hi)
        give(q, S_YB, sib, shard, hi)

    def corner_down(q):
        shard = at(ym, xo, c)
        got(q, YP_X, shard, but_first)
        got(q, X_P, shard, first)
        give(q, S_YPX, sib, shard)

    def corner_up(q):
        shard = at(yp, xo, c)
        got(q, YM_X, shard, but_last)
        got(q, X_M, shard, last)
        give(q, S_YMX, sib, shard)

    def cross_lo(q):
        shard = at(y2, xo, c)
        got(q, X_FA, shard, lo)
        give(q, S_XA, sib, shard, lo)

    def cross_hi(q):
        shard = at(y2, xo, c)
        got(q, X_FB, shard, hi)
        give(q, S_XB, sib, shard, hi)

    near, distant = [(y, x), (ym, x), (yp, x), (y, xo)], [(y2, x), (ym, xo), (yp, xo), (y2, xo)]

    def product(q, chips, core):
        s = None
        for yy, xx in chips:
            i = at(yy, xx, core)
            cols = pl.ds(pl.multiple_of(i * rows, rows), rows)
            d = jnp.dot(xv[:, cols], wg[q, i], preferred_element_type=F32)
            s = d if s is None else s + d
        return s

    def keys_a(q):
        acc[q] = product(q, near, c)

    def keys_b(q):
        got(q, S_OWN, at(y, x, co))
        got(q, S_X, at(y, xo, co))
        got(q, S_YP, at(ym, x, co))
        got(q, S_YM, at(yp, x, co))
        acc[q] += product(q, near, co)

    def keys_c(q):
        acc[q] += product(q, distant, c)

    resid = {}

    def keys_d(q):
        got(q, S_YA, at(y2, x, co), lo)
        got(q, S_YB, at(y2, x, co), hi)
        got(q, S_YPX, at(ym, xo, co))
        got(q, S_YMX, at(yp, xo, co))
        got(q, S_XA, at(y2, xo, co), lo)
        got(q, S_XB, at(y2, xo, co), hi)
        keys = (acc[q] + product(q, distant, co)) * scale
        target = tv[:, columns(q)].astype(F32)
        resid[q] = (live[...] * (keys - target) / total[0:1, 0:1]).astype(BF16)

    def turn(i):
        for k in (2 * i, 2 * i + 1):
            xt[k] = jnp.transpose(xv[:, k * rows:(k + 1) * rows])

    order = [(y2, xo), (yp, xo), (ym, xo), (y2, x), (yp, x), (ym, x), (y, xo), (y, x)]

    def slope(j, core, q):
        yy, xx = order[j]
        return jnp.dot(xt[at(yy, xx, core)], resid[q], preferred_element_type=F32)

    def theirs(j, q):
        gsend[q, j] = slope(j, co, q).astype(BF16)
        send(gsend.at[q, j], gsib.at[q, j], q, GS + j, sib)

    def ours(j, q):
        gown[q, j] = slope(j, c, q)

    def pair(q, j, rng=every):
        return gown[q, j, rng] + gsib[q, j, rng].astype(F32)

    def pass_on(q, buf, dst, rng, value, kind, peer):
        buf[q, rng] = value.astype(BF16)
        send(buf.at[q, rng], dst.at[q, rng], q, kind, peer)

    def sum_cross(q):
        arrived(gsib.at[q, 0], q, GS)
        pass_on(q, tx1, rx1, every, pair(q, 0), X1, side)

    def sum_corner_up(q):
        arrived(gsib.at[q, 1], q, GS + 1)
        ty1p[q] = pair(q, 1).astype(BF16)
        send(ty1p.at[q, but_first], ry1p.at[q, but_first], q, Y1P, up)
        send(ty1p.at[q, first], rxep.at[q], q, XEP, side)

    def sum_corner_down(q):
        arrived(gsib.at[q, 2], q, GS + 2)
        ty1m[q] = pair(q, 2).astype(BF16)
        send(ty1m.at[q, but_last], ry1m.at[q, but_last], q, Y1M, down)
        send(ty1m.at[q, last], rxem.at[q], q, XEM, side)

    def sum_up(q):
        arrived(gsib.at[q, 4], q, GS + 4)
        pass_on(q, ty3p, ry3p, hi, pair(q, 4, hi), Y3PB, up)

    def sum_down(q):
        arrived(gsib.at[q, 5], q, GS + 5)
        pass_on(q, ty3m, ry3m, lo, pair(q, 5, lo), Y3MA, down)

    def sum_far(q):
        arrived(gsib.at[q, 3], q, GS + 3)
        arrived(rx1.at[q], q, X1)
        s = pair(q, 3) + rx1[q].astype(F32)
        pass_on(q, ty2p, ry2p, pl.ds(0, half), s[:half], Y2P, up)
        pass_on(q, ty2m, ry2m, pl.ds(0, half), s[half:], Y2M, down)

    def sum_side(q):
        arrived(gsib.at[q, 6], q, GS + 6)
        arrived(ry1p.at[q, but_first], q, Y1P)
        arrived(ry1m.at[q, but_last], q, Y1M)
        s = pair(q, 6)
        zero = jnp.zeros((edge, cw), F32)
        s = s + jnp.concatenate([zero, ry1p[q, but_first].astype(F32)])
        s = s + jnp.concatenate([ry1m[q, but_last].astype(F32), zero])
        pass_on(q, tx2, rx2, every, s, X2, side)

    def sum_up_far(q):
        arrived(ry2p.at[q], q, Y2P)
        arrived(rxep.at[q], q, XEP)
        s = pair(q, 4, lo) + ry2p[q].astype(F32)
        s = s + jnp.concatenate([rxep[q].astype(F32), jnp.zeros((half - edge, cw), F32)])
        pass_on(q, ty3p, ry3p, lo, s, Y3PA, up)

    def sum_down_far(q):
        arrived(ry2m.at[q], q, Y2M)
        arrived(rxem.at[q], q, XEM)
        s = pair(q, 5, hi) + ry2m[q].astype(F32)
        s = s + jnp.concatenate([jnp.zeros((half - edge, cw), F32), rxem[q].astype(F32)])
        pass_on(q, ty3m, ry3m, hi, s, Y3MB, down)

    def finish(q):
        arrived(gsib.at[q, 7], q, GS + 7)
        arrived(rx2.at[q], q, X2)
        arrived(ry3p.at[q, hi], q, Y3PB)
        arrived(ry3m.at[q, lo], q, Y3MA)
        arrived(ry3p.at[q, lo], q, Y3PA)
        arrived(ry3m.at[q, hi], q, Y3MB)
        s = pair(q, 7) + rx2[q].astype(F32) + ry3p[q].astype(F32) + ry3m[q].astype(F32)
        grad_out[:, columns(q)] = s * scale

    pl.semaphore_wait(barrier, len(peers))
    own(0)
    count(0)
    count(1)
    own(1)
    own(2)
    from_up(0)
    l_act.wait()
    turn(6)
    from_down(0)
    from_up(1)
    count(2)
    turn(5)
    from_side(0)
    keys_a(0)
    from_down(1)
    own(3)
    from_down(2)
    mean_start()
    far_lo(0)
    count(3)
    far_hi(0)
    turn(0)
    from_up(2)
    from_side(1)
    from_side(2)
    turn(7)
    turn(1)
    keys_a(2)
    far_hi(1)
    corner_down(0)
    keys_b(0)
    keys_a(1)
    far_lo(1)
    keys_b(2)
    turn(4)
    cross_lo(0)
    corner_up(0)
    turn(2)
    keys_b(1)
    cross_hi(0)
    from_up(3)
    turn(3)
    from_down(3)
    count(4)
    keys_c(0)
    from_side(3)
    far_lo(2)
    cross_hi(1)
    l_tgt.wait()
    keys_d(0)
    theirs(0, 0)
    theirs(1, 0)
    ours(0, 0)
    far_hi(2)
    keys_a(3)
    theirs(2, 0)
    ours(2, 0)
    sum_cross(0)
    corner_up(1)
    cross_lo(1)
    corner_down(1)
    keys_c(1)
    ours(3, 0)
    ours(4, 0)
    ours(1, 0)
    theirs(3, 0)
    sum_corner_down(0)
    theirs(4, 0)
    sum_corner_up(0)
    corner_down(2)
    corner_up(2)
    keys_d(1)
    theirs(0, 1)
    ours(1, 1)
    theirs(5, 0)
    cross_hi(2)
    cross_lo(2)
    far_hi(3)
    keys_c(2)
    theirs(1, 1)
    ours(5, 1)
    ours(5, 0)
    far_lo(3)
    ours(0, 1)
    theirs(2, 1)
    keys_d(2)
    sum_far(0)
    corner_up(3)
    sum_cross(1)
    theirs(0, 2)
    sum_corner_up(1)
    sum_down(0)
    theirs(1, 2)
    theirs(3, 1)
    ours(2, 2)
    ours(2, 1)
    sum_corner_down(1)
    ours(4, 2)
    ours(4, 1)
    sum_up(0)
    theirs(2, 2)
    corner_down(3)
    theirs(4, 1)
    ours(3, 1)
    keys_b(3)
    cross_hi(3)
    cross_lo(3)
    theirs(5, 1)
    keys_c(3)
    mean_sum()
    sum_corner_down(2)
    ours(0, 2)
    sum_cross(2)
    sum_up(1)
    ours(1, 2)
    keys_d(3)
    sum_up_far(0)
    theirs(0, 3)
    sum_down_far(0)
    ours(5, 3)
    ours(1, 3)
    ours(0, 3)
    sum_far(1)
    theirs(6, 1)
    theirs(3, 2)
    ours(5, 2)
    theirs(4, 2)
    theirs(6, 0)
    sum_cross(3)
    theirs(5, 2)
    ours(7, 3)
    sum_corner_up(2)
    ours(6, 0)
    mean_share()
    sum_down(1)
    theirs(1, 3)
    ours(2, 3)
    ours(6, 2)
    ours(7, 1)
    ours(3, 2)
    sum_far(2)
    theirs(2, 3)
    theirs(6, 2)
    sum_side(0)
    theirs(3, 3)
    sum_corner_up(3)
    theirs(4, 3)
    ours(3, 3)
    ours(6, 1)
    sum_up_far(1)
    theirs(5, 3)
    sum_corner_down(3)
    settle_gather()
    sum_far(3)
    theirs(6, 3)
    sum_down_far(1)
    theirs(7, 1)
    sum_up(2)
    ours(6, 3)
    theirs(7, 3)
    ours(4, 3)
    sum_side(1)
    sum_side(3)
    sum_down(3)
    ours(7, 2)
    sum_down_far(3)
    mean_end()
    sum_up(3)
    sum_up_far(3)
    sum_down(2)
    sum_up_far(2)
    sum_side(2)
    sum_down_far(2)
    ours(7, 0)
    theirs(7, 0)
    finish(1)
    settle(1)
    theirs(7, 2)
    finish(0)
    settle(0)
    finish(3)
    settle(3)
    finish(2)
    for tag in list(sends):
        settle(tag)


def sync(activations, targets, token_ids, sync_fragment, params, anchor):
    tokens, width = activations.shape[1:]
    rows, kv = params.shape[1:]
    nq = kv // HEAD
    edge = EDGE * rows // 512
    piece = pltpu.VMEM((nq, rows, HEAD), BF16)
    part = pltpu.VMEM((nq, rows // 2, HEAD), BF16)
    thin = pltpu.VMEM((nq, edge, HEAD), BF16)
    block = pltpu.VMEM((rows // NZ, HEAD), F32)
    hbm = pl.BlockSpec(memory_space=pltpu.HBM)
    vmem = pl.BlockSpec(memory_space=pltpu.VMEM)
    return pl.pallas_call(
        functools.partial(sync_kernel, float(width) ** (-0.5)),
        out_shape=(jax.ShapeDtypeStruct((rows, kv), F32), jax.ShapeDtypeStruct((NZ, rows // NZ, HEAD), F32)),
        in_specs=[hbm] * 6,
        out_specs=(vmem, vmem),
        scratch_shapes=[
            pltpu.SMEM(sync_fragment.shape, jnp.int32),
            pltpu.VMEM((tokens, width), BF16),
            pltpu.VMEM((NF, rows, tokens), BF16),
            pltpu.VMEM((tokens, kv), BF16),
            pltpu.VMEM((rows, kv), F32),
            pltpu.VMEM((rows, kv), F32),
            pltpu.VMEM((1, tokens), jnp.int32),
            pltpu.VMEM((tokens, HEAD), F32),
            pltpu.VMEM((8, HEAD), F32),
            pltpu.VMEM((nq, NF, rows, HEAD), BF16),
            pltpu.VMEM((nq, tokens, HEAD), F32),
            pltpu.VMEM((nq, 8, rows, HEAD), F32),
            pltpu.VMEM((nq, 8, rows, HEAD), BF16),
            pltpu.VMEM((nq, 8, rows, HEAD), BF16),
            piece, piece, piece, thin, thin, part, part, piece, piece, piece,
            piece, piece, piece, part, part, piece, piece, piece,
            pltpu.VMEM((NZ, rows // NZ, HEAD), F32),
            pltpu.VMEM((NZ - 1, rows // NZ, HEAD), F32),
            block, block,
            pltpu.VMEM((4, 8, HEAD), F32),
            pltpu.VMEM((4, 8, HEAD), F32),
            pltpu.SemaphoreType.DMA((nq, KINDS)),
            pltpu.SemaphoreType.DMA((nq, KINDS)),
            pltpu.SemaphoreType.DMA((2 * NZ,)),
            pltpu.SemaphoreType.DMA((2 * NZ,)),
            pltpu.SemaphoreType.DMA((4,)),
            pltpu.SemaphoreType.DMA((4,)),
            pltpu.SemaphoreType.DMA((nq + 5,)),
        ],
        compiler_params=pltpu.CompilerParams(
            collective_id=0, has_side_effects=True, vmem_limit_bytes=46 * 2**20
        ),
        cost_estimate=pl.CostEstimate(
            flops=4 * tokens * width * kv, bytes_accessed=2 * tokens * width + 12 * rows * kv, transcendentals=0
        ),
        name="sync",
    )(*[
        pltpu.with_memory_space_constraint(a, pltpu.HBM)
        for a in (activations, targets, token_ids, sync_fragment, params, anchor)
    ])


def update_kernel(steps, frag, grad, delta, params, adam_m, adam_v, anchor, momentum,
                  out_params, out_m, out_v, out_anchor, out_momentum,
                  new_params, new_m, new_v, new_anchor, new_momentum, sem):
    rows = grad.shape[0]
    size = rows // steps
    copies = []

    def store(src, dst):
        copy = pltpu.make_async_copy(src, dst, sem.at[len(copies)])
        copy.start()
        copies.append(copy)

    fragment = pl.ds(pl.multiple_of(frag[0] * HEAD, HEAD), HEAD)
    arriving = pl.ds(pl.multiple_of(frag[1] * HEAD, HEAD), HEAD)
    for i in range(steps):
        r = pl.ds(i * size, size)
        slope = grad[r]
        weight = params[0, r]
        first = beta_one * adam_m[0, r] + (1.0 - beta_one) * slope
        second = beta_two * adam_v[0, r] + (1.0 - beta_two) * slope * slope
        new_m[r] = first
        store(new_m.at[r], out_m.at[0, r])
        new_v[r] = second
        store(new_v.at[r], out_v.at[0, r])
        new_params[r] = weight - learn_rate * (first / (jnp.sqrt(second) + adam_epsilon) + decay_rate * weight)
        new_params[r, arriving] = merge_weight * new_params[r, arriving] + (1.0 - merge_weight) * anchor[r, arriving]
        store(new_params.at[r], out_params.at[0, r])
        new_anchor[r] = anchor[r]
        new_momentum[r] = momentum[r]
        change = delta[r]
        moment = outer_beta * momentum[r, fragment] + change
        new_momentum[r, fragment] = moment
        store(new_momentum.at[r], out_momentum.at[r])
        new_anchor[r, fragment] = anchor[r, fragment] - outer_rate * (change + outer_beta * moment)
        store(new_anchor.at[r], out_anchor.at[r])
    for copy in copies:
        copy.wait()


def update(frag, grad, delta, params, adam_m, adam_v, anchor, momentum, steps=4):
    rows, kv = grad.shape
    vmem = pl.BlockSpec(memory_space=pltpu.VMEM)
    hbm = pl.BlockSpec(memory_space=pltpu.HBM)
    return pl.pallas_call(
        functools.partial(update_kernel, steps),
        out_shape=[jax.ShapeDtypeStruct((1, rows, kv), F32)] * 3 + [jax.ShapeDtypeStruct((rows, kv), F32)] * 2,
        in_specs=[pl.BlockSpec(memory_space=pltpu.SMEM)] + [vmem] * 7,
        out_specs=[hbm] * 5,
        scratch_shapes=[pltpu.VMEM((rows, kv), F32)] * 5 + [pltpu.SemaphoreType.DMA((5 * steps,))],
        compiler_params=pltpu.CompilerParams(vmem_limit_bytes=16 * 2**20),
        name="update",
    )(frag, grad, delta, params, adam_m, adam_v, anchor, momentum)


def on_device(activations, targets, token_ids, sync_fragment, params, adam_m, adam_v, anchor, momentum):
    grad, delta = sync(activations, targets, token_ids, sync_fragment, params, anchor)
    delta = delta.reshape(delta.shape[0] * delta.shape[1], delta.shape[2])
    return tuple(update(sync_fragment, grad, delta, params, adam_m, adam_v, anchor, momentum))


def solution(mesh):
    worker = P("group", "fsdp", None)
    shared = P("fsdp", None)
    return jax.shard_map(
        on_device,
        mesh=mesh,
        in_specs=(worker, worker, P("group", "fsdp"), P(), worker, worker, worker, shared, shared),
        out_specs=(worker, worker, worker, shared, shared),
        check_vma=False,
    )
```

time: 295 us -> 73 us (0.25)
  the two profiles are of different devices: /device:TPU:160 before, /device:TPU:1 now
where the time goes in v2:
time: 73 us; the launch traced here: 72.9 us
  Pallas kernels  72 us (99%)
  between operations  0.9 us (1%)
    pallas_call x1, Pallas kernels, sync(): pl.pallas_call(functools.partial(sync_kernel, float(width) ** (-0.5)), ou...  68.8 us
    pallas_call x1, Pallas kernels, update(): pl.pallas_call(functools.partial(update_kernel, steps), out_shape=[jax.Sh...  3.17 us

profile of v2, /device:TPU:1, one launch (start us, length us, event | category | flops | bytes accessed | tf_op | source)
XLA Modules:
  0.0 72.9 jit_solution(4359741550902639584)
XLA Ops:
  0.6 0.0 copy-start.1
  0.6 0.0 copy-start
  0.7 0.0 copy-start.5
  0.7 0.0 copy-start.4
  0.7 0.0 copy-start.3
  0.7 0.0 copy-start.2
  0.7 68.8 %sync.1 = (f32[512,512]{1,0:T(8,128)S(1)}, f32[8,64,128]{2,1,0:T(8,128)S(1)}) custom-call(bf16[1,256,8192]{2,1,0:T(8,128)(2,1)} %act.1, bf16[1,256,512]{2,1,0:T(8,128)(2,1)} %tgt.1, s32[1,256]{1,0:T(1,128)} %ids.1, s32[4]{0:T(128)} %frag.1, f32[1,512,512]{2,1,0:T(8,128)} %params.3, f32[512,512]{1,0:T(8,128)} %anchor.3), custom_call_target="tpu_custom_call" | custom-call | flops 4294967296 | bytes 7340032 | tf_op jit(solution)/shard_map/sync/pallas_call | solution.py:571
  69.5 0.0 copy-done.1
  69.5 0.0 copy-done
  69.5 0.0 copy-done.5
  69.5 0.0 copy-done.4
  69.5 0.0 copy-done.3
  69.6 0.0 copy-done.2
  69.6 3.2 %update.1 = (f32[1,512,512]{2,1,0:T(8,128)}, f32[1,512,512]{2,1,0:T(8,128)}, f32[1,512,512]{2,1,0:T(8,128)}, f32[512,512]{1,0:T(8,128)}, f32[512,512]{1,0:T(8,128)}) custom-call(s32[4]{0:T(128)S(1)} %copy-done.5, f32[512,512]{1,0:T(8,128)S(1)} %get-tuple-element.7.grad, f32[512,128]{1,0:T(8,128)S(1)} %bitcast.1, f32[1,512,512]{2,1,0:T(8,128)S(1)} %copy-done, ...), custom_call_target="tpu_custom_call" | custom-call | tf_op jit(solution)/shard_map/update/pallas_call | solution.py:662
Async XLA Ops:
  0.6 68.9 %copy-start.1 = (f32[512,512]{1,0:T(8,128)S(1)}, f32[512,512]{1,0:T(8,128)}, u32[]{:S(2)}) copy-start(f32[512,512]{1,0:T(8,128)} %anchor.3) | copy-start | bytes 3145732
  0.6 68.9 %copy-start = (f32[1,512,512]{2,1,0:T(8,128)S(1)}, f32[1,512,512]{2,1,0:T(8,128)}, u32[]{:S(2)}) copy-start(f32[1,512,512]{2,1,0:T(8,128)} %params.3) | copy-start | bytes 3145732
  0.7 68.9 %copy-start.5 = (s32[4]{0:T(128)S(1)}, s32[4]{0:T(128)}, u32[]{:S(2)}) copy-start(s32[4]{0:T(128)} %frag.1) | copy-start | bytes 52
  0.7 68.9 %copy-start.4 = (f32[512,512]{1,0:T(8,128)S(1)}, f32[512,512]{1,0:T(8,128)}, u32[]{:S(2)}) copy-start(f32[512,512]{1,0:T(8,128)} %momentum.1) | copy-start | bytes 3145732
  0.7 68.9 %copy-start.3 = (f32[1,512,512]{2,1,0:T(8,128)S(1)}, f32[1,512,512]{2,1,0:T(8,128)}, u32[]{:S(2)}) copy-start(f32[1,512,512]{2,1,0:T(8,128)} %adam_v.1) | copy-start | bytes 3145732
  0.7 68.9 %copy-start.2 = (f32[1,512,512]{2,1,0:T(8,128)S(1)}, f32[1,512,512]{2,1,0:T(8,128)}, u32[]{:S(2)}) copy-start(f32[1,512,512]{2,1,0:T(8,128)} %adam_m.1) | copy-start | bytes 3145732

commit v3 on v2

v3 whole, which is shorter than its diff:
```python
import functools

import jax
import jax.numpy as jnp
from jax import lax
from jax.experimental import pallas as pl
from jax.experimental.pallas import tpu as pltpu
from jax.sharding import PartitionSpec as P

HEAD = 128
MESH = pl.DeviceIdType.MESH
F32 = jnp.float32
BF16 = jnp.bfloat16

beta_one = 0.9
beta_two = 0.999
learn_rate = 0.05
decay_rate = 0.1
adam_epsilon = 1e-08
outer_rate = 0.7
outer_beta = 0.9
merge_weight = 0.5

NF = 16
NZ = 8

EDGE = 80

(X_OWN, YP_OWN, YM_OWN, YP_X, YM_X, YP_F, YM_F, X_P, X_M, X_FA, X_FB, KEYS, ROWS,
 X1, Y1P, Y1M, XEP, XEM, Y2P, Y2M, Y3PB, Y3PA, Y3MA, Y3MB, X2) = range(25)
KINDS = 25


def sync_kernel(scale, act, tgt, ids, fragments, params, adam_m, adam_v, anchor, momentum,
                grad_out, delta_out, pv, mv, vv, av, uv,
                frag, xk, xt, tv, iv, live, total, wg, acc, ksend, krecv, rs, gown,
                rx1, ry1p, ry1m, rxep, rxem, ry2p, ry2m, ry3p, ry3m, rx2,
                tx1, ty1p, ty1m, ty2p, ty2m, ty3p, ty3m, tx2,
                dd, sum_b, sum_c, sum_d, from_b, from_c, from_d, from_e, cs, cr,
                ssem, rsem, zsem, zrsem, csem, crsem, xsem, xrsem, lsem):
    nq, _, rows, cw = wg.shape
    tokens = iv.shape[1]
    half = rows // 2
    edge = rxep.shape[1]
    g, me = lax.axis_index("group"), lax.axis_index("fsdp")
    y, x, c = me // 4, lax.rem(me // 2, 2), lax.rem(me, 2)
    z, far = lax.rem(g, NZ), g // NZ
    yp, ym, y2, xo, co = lax.rem(y + 1, 4), lax.rem(y + 3, 4), lax.rem(y + 2, 4), 1 - x, 1 - c
    groups = lax.axis_size("group")

    def at(yy, xx, cc):
        return yy * 4 + xx * 2 + cc

    def chip(yy, xx):
        return yy * 2 + xx

    sib, up, down, side = ((g, at(y, x, co)), (g, at(yp, x, c)), (g, at(ym, x, c)), (g, at(y, xo, c)))

    b0, b1, b2 = lax.rem(z, 2), lax.rem(z // 2, 2), z // 4
    flip0, flip1, flip2, across = ((g + 1 - 2 * b0, me), (g + 2 - 4 * b1, me), (g + 4 - 8 * b2, me), (g + 8 - 16 * far, me))
    partners = [flip0, flip1, flip2, across] if groups > 1 else []
    odd = lax.rem(b0 + b1 + far, 2)
    lower = (1 - b2) * (b0 + b1 + far) + b2 * (1 + 3 * odd)

    neighbours = [sib, up, down, side]
    barrier = pltpu.get_barrier_semaphore()

    def greet(peers):
        for peer in peers:
            pl.semaphore_signal(barrier, inc=1, device_id=peer, device_id_type=MESH)

    greet(neighbours)

    def columns(q):
        return slice(q * cw, (q + 1) * cw)

    def load(src, dst, k):
        copy = pltpu.make_async_copy(src, dst, lsem.at[k])
        copy.start()
        return copy

    l_params = [load(params.at[0, :, columns(q)], pv.at[:, columns(q)], q) for q in range(nq)]
    l_ids = load(ids, iv, nq)

    def block(k, core):
        return act.at[0, :, pl.ds(pl.multiple_of((2 * k + core) * rows, rows), rows)]

    def held(half, k):
        return xk.at[pl.ds(half * tokens, tokens), pl.ds(k * rows, rows)]

    l_act = [load(block(k, c), held(0, k), nq + 8 + k) for k in range(NF // 2)]
    l_tgt = load(tgt.at[0], tv, nq + 2)
    l_anchor = load(anchor, av, nq + 3)
    l_frag = load(fragments, frag, nq + 4)
    l_later = [load(adam_m.at[0], mv, nq + 5), load(adam_v.at[0], vv, nq + 6), load(momentum, uv, nq + 7)]

    sends = {}

    def start(copy, tag=None):
        copy.start()
        sends.setdefault(tag, []).append(copy)

    def settle(tag):
        for copy in sends.pop(tag, []):
            copy.wait_send()

    def settle_gather():
        for q in range(nq):
            settle(-1 - q)

    def remote(src, dst, q, kind, peer):
        return pltpu.make_async_remote_copy(
            src_ref=src, dst_ref=dst, send_sem=ssem.at[q, kind], recv_sem=rsem.at[q, kind],
            device_id=peer, device_id_type=MESH)

    def send(src, dst, q, kind, peer):
        start(remote(src, dst, q, kind, peer), q if kind >= X1 else -1 - q)

    def arrived(dst, q, kind):
        remote(dst, dst, q, kind, sib).wait_recv()

    y1, y3 = y + 1 - 2 * lax.rem(y, 2), 3 - y
    count_peers = [sib, side, (g, at(y1, x, c)), (g, at(y3, x, c))]

    def count_copy(k):
        return pltpu.make_async_remote_copy(
            src_ref=cs.at[k], dst_ref=cr.at[k], send_sem=csem.at[k], recv_sem=crsem.at[k],
            device_id=count_peers[k], device_id_type=MESH)

    def count(k):
        if k == 0:
            l_ids.wait()
            row = jnp.where(iv[...] != 0, 1.0, 0.0).astype(F32)
            live[...] = jnp.transpose(jnp.broadcast_to(row, (HEAD, tokens)))
            part = jnp.broadcast_to(jnp.sum(row), cs.shape[1:])
        else:
            count_copy(k - 1).wait_recv()
            part = cs[k - 1] + cr[k - 1]
        if k < 4:
            cs[k] = part
            start(count_copy(k))
        else:
            total[...] = part

    def zcopy(src, dst, k, peer):
        return pltpu.make_async_remote_copy(
            src_ref=src, dst_ref=dst, send_sem=zsem.at[k], recv_sem=zrsem.at[k],
            device_id=peer, device_id_type=MESH)

    def mean_start():
        l_anchor.wait()
        l_frag.wait()
        diff = av[:, columns(0)] - pv[:, columns(0)]
        for f in range(1, nq):
            diff = jnp.where(jnp.full(diff.shape, frag[0]) == f, av[:, columns(f)] - pv[:, columns(f)], diff)
        dd[...] = diff.reshape(dd.shape)
        if groups > 1:
            @pl.when(lower < 4)
            def _():
                pl.semaphore_wait(barrier, 4 - lower)

            start(zcopy(dd.at[pl.ds(2 - 2 * b0, 2)], from_b, 0, flip0))

    def mean_b():
        if groups > 1:
            zcopy(from_b, from_b, 0, flip0).wait_recv()
            sum_b[...] = dd[pl.ds(2 * b0, 2)] + from_b[...]
            start(zcopy(sum_b.at[1 - b1], from_c, 1, flip1))

    def mean_c():
        if groups > 1:
            zcopy(from_c, from_c, 1, flip1).wait_recv()
            sum_c[...] = sum_b[b1] + from_c[...]
            start(zcopy(sum_c, from_d, 2, across))

    def mean_d():
        if groups > 1:
            zcopy(from_d, from_d, 2, across).wait_recv()
            sum_d[...] = sum_c[...] + from_d[...]
            start(zcopy(sum_d, from_e, 3, flip2))

    mine, other = 2 * b0 + b1, 2 * b0 + 1 - b1

    def mean_e():
        if groups > 1:
            zcopy(from_e, from_e, 3, flip2).wait_recv()
            delta_out[mine] = (sum_d[...] + from_e[...]) / groups
            start(zcopy(delta_out.at[mine], delta_out.at[mine], 4, flip1))

    def mean_f():
        if groups > 1:
            zcopy(delta_out.at[other], delta_out.at[other], 4, flip1).wait_recv()
            half_done = delta_out.at[pl.ds(2 * b0, 2)]
            start(zcopy(half_done, half_done, 5, flip0))

    def mean_end():
        if groups > 1:
            half_done = delta_out.at[pl.ds(2 - 2 * b0, 2)]
            zcopy(half_done, half_done, 5, flip0).wait_recv()
        else:
            delta_out[...] = dd[...]

    def swap(k):
        return pltpu.make_async_remote_copy(
            src_ref=block(k, co), dst_ref=held(1, k), send_sem=xsem.at[k], recv_sem=xrsem.at[k],
            device_id=sib, device_id_type=MESH)

    def swap_start():
        for k in range(NF // 2):
            start(swap(k))

    def swap_end():
        for k in range(NF // 2):
            l_act[k].wait()
            swap(k).wait_recv()

    every, lo, hi = pl.ds(0, rows), pl.ds(0, half), pl.ds(half, half)
    first, but_first = pl.ds(0, edge), pl.ds(edge, rows - edge)
    last, but_last = pl.ds(rows - edge, edge), pl.ds(0, rows - edge)

    def give(q, kind, peer, shard, rng=every):
        ref = wg.at[q, shard, rng]
        send(ref, ref, q, kind, peer)

    def got(q, kind, shard, rng=every):
        arrived(wg.at[q, shard, rng], q, kind)

    def cast(q):
        l_params[q].wait()
        wg[q, chip(y, x)] = pv[:, columns(q)].astype(BF16)

    def own(q):
        if q > 0:
            cast(q)
        shard = chip(y, x)
        give(q, X_OWN, side, shard)
        give(q, YP_OWN, up, shard)
        give(q, YM_OWN, down, shard)

    def from_side(q):
        shard = chip(y, xo)
        got(q, X_OWN, shard)
        give(q, YP_X, up, shard, but_first)
        give(q, YM_X, down, shard, but_last)

    def from_down(q):
        shard = chip(ym, x)
        got(q, YP_OWN, shard)
        give(q, YP_F, up, shard, lo)
        give(q, X_P, side, shard, first)

    def from_up(q):
        shard = chip(yp, x)
        got(q, YM_OWN, shard)
        give(q, YM_F, down, shard, hi)
        give(q, X_M, side, shard, last)

    def far_lo(q):
        shard = chip(y2, x)
        got(q, YP_F, shard, lo)
        give(q, X_FA, side, shard, lo)

    def far_hi(q):
        shard = chip(y2, x)
        got(q, YM_F, shard, hi)
        give(q, X_FB, side, shard, hi)

    def product(q, chips):
        s = None
        for yy, xx in chips:
            k = chip(yy, xx)
            cols = pl.ds(pl.multiple_of(k * rows, rows), rows)
            d = jnp.dot(xk[:, cols], wg[q, k], preferred_element_type=F32)
            s = d if s is None else s + d
        return s

    def keys_a(q):
        acc[q] = product(q, [(y, x), (ym, x), (yp, x), (y, xo)])

    def keys_b(q):
        got(q, YP_X, chip(ym, xo), but_first)
        got(q, X_P, chip(ym, xo), first)
        got(q, YM_X, chip(yp, xo), but_last)
        got(q, X_M, chip(yp, xo), last)
        got(q, X_FA, chip(y2, xo), lo)
        got(q, X_FB, chip(y2, xo), hi)
        s = acc[q] + product(q, [(y2, x), (ym, xo), (yp, xo), (y2, xo)])
        acc[q] = s
        ksend[q] = s[tokens:]
        send(ksend.at[q], krecv.at[q], q, KEYS, sib)

    def residual(q):
        arrived(krecv.at[q], q, KEYS)
        keys = (acc[q, :tokens] + krecv[q]) * scale
        target = tv[:, columns(q)].astype(F32)
        rs[q, :tokens] = (live[...] * (keys - target) / total[0:1, 0:1]).astype(BF16)
        send(rs.at[q, pl.ds(0, tokens)], rs.at[q, pl.ds(tokens, tokens)], q, ROWS, sib)

    def turn(k):
        xt[k] = jnp.transpose(xk[:, k * rows:(k + 1) * rows])

    ready = set()

    def slope(q, yy, xx):
        if q not in ready:
            ready.add(q)
            arrived(rs.at[q, pl.ds(tokens, tokens)], q, ROWS)
        return jnp.dot(xt[chip(yy, xx)], rs[q], preferred_element_type=F32)

    def pass_on(q, buf, dst, rng, value, kind, peer):
        buf[q, rng] = value.astype(BF16)
        send(buf.at[q, rng], dst.at[q, rng], q, kind, peer)

    def sum_cross(q):
        pass_on(q, tx1, rx1, every, slope(q, y2, xo), X1, side)

    def sum_corner_up(q):
        ty1p[q] = slope(q, yp, xo).astype(BF16)
        send(ty1p.at[q, but_first], ry1p.at[q, but_first], q, Y1P, up)
        send(ty1p.at[q, first], rxep.at[q], q, XEP, side)

    def sum_corner_down(q):
        ty1m[q] = slope(q, ym, xo).astype(BF16)
        send(ty1m.at[q, but_last], ry1m.at[q, but_last], q, Y1M, down)
        send(ty1m.at[q, last], rxem.at[q], q, XEM, side)

    def sum_up(q):
        gown[q, 0] = slope(q, yp, x)
        pass_on(q, ty3p, ry3p, hi, gown[q, 0, hi], Y3PB, up)

    def sum_down(q):
        gown[q, 1] = slope(q, ym, x)
        pass_on(q, ty3m, ry3m, lo, gown[q, 1, lo], Y3MA, down)

    def part_far(q):
        gown[q, 2] = slope(q, y2, x)

    def part_side(q):
        gown[q, 3] = slope(q, y, xo)

    def part_own(q):
        gown[q, 4] = slope(q, y, x)

    def sum_far(q):
        arrived(rx1.at[q], q, X1)
        s = gown[q, 2] + rx1[q].astype(F32)
        pass_on(q, ty2p, ry2p, pl.ds(0, half), s[:half], Y2P, up)
        pass_on(q, ty2m, ry2m, pl.ds(0, half), s[half:], Y2M, down)

    def sum_side(q):
        arrived(ry1p.at[q, but_first], q, Y1P)
        arrived(ry1m.at[q, but_last], q, Y1M)
        zero = jnp.zeros((edge, cw), F32)
        s = gown[q, 3] + jnp.concatenate([zero, ry1p[q, but_first].astype(F32)])
        s = s + jnp.concatenate([ry1m[q, but_last].astype(F32), zero])
        pass_on(q, tx2, rx2, every, s, X2, side)

    def sum_up_far(q):
        arrived(ry2p.at[q], q, Y2P)
        arrived(rxep.at[q], q, XEP)
        s = gown[q, 0, lo] + ry2p[q].astype(F32)
        s = s + jnp.concatenate([rxep[q].astype(F32), jnp.zeros((half - edge, cw), F32)])
        pass_on(q, ty3p, ry3p, lo, s, Y3PA, up)

    def sum_down_far(q):
        arrived(ry2m.at[q], q, Y2M)
        arrived(rxem.at[q], q, XEM)
        s = gown[q, 1, hi] + ry2m[q].astype(F32)
        s = s + jnp.concatenate([jnp.zeros((half - edge, cw), F32), rxem[q].astype(F32)])
        pass_on(q, ty3m, ry3m, hi, s, Y3MB, down)

    def finish(q):
        arrived(rx2.at[q], q, X2)
        arrived(ry3p.at[q, hi], q, Y3PB)
        arrived(ry3m.at[q, lo], q, Y3MA)
        arrived(ry3p.at[q, lo], q, Y3PA)
        arrived(ry3m.at[q, hi], q, Y3MB)
        s = gown[q, 4] + rx2[q].astype(F32) + ry3p[q].astype(F32) + ry3m[q].astype(F32)
        grad_out[:, columns(q)] = s * scale

    cast(0)
    pl.semaphore_wait(barrier, len(neighbours) + (lower if groups > 1 else 0))
    greet(partners)
    own(0)
    own(1)
    count(0)
    count(1)
    own(2)
    swap_start()
    swap_end()
    from_up(1)
    count(2)
    turn(5)
    from_down(0)
    from_up(0)
    own(3)
    turn(4)
    mean_start()
    far_lo(0)
    from_up(2)
    from_down(1)
    turn(2)
    far_hi(0)
    from_down(2)
    far_hi(1)
    count(3)
    from_side(0)
    from_side(1)
    from_down(3)
    from_side(2)
    mean_b()
    keys_a(2)
    far_lo(1)
    keys_a(0)
    turn(6)
    from_up(3)
    keys_a(1)
    turn(0)
    count(4)
    far_hi(2)
    far_lo(2)
    turn(3)
    from_side(3)
    turn(7)
    turn(1)
    keys_b(0)
    l_tgt.wait()
    residual(0)
    mean_c()
    keys_b(1)
    sum_cross(0)
    sum_corner_up(0)
    residual(1)
    far_hi(3)
    sum_corner_down(0)
    sum_up(0)
    far_lo(3)
    part_own(0)
    sum_down(1)
    keys_b(2)
    mean_d()
    sum_corner_up(1)
    sum_down(0)
    residual(2)
    sum_cross(1)
    sum_corner_down(1)
    keys_a(3)
    sum_corner_down(2)
    sum_down(2)
    sum_up(1)
    sum_cross(2)
    part_far(1)
    sum_up(2)
    part_side(1)
    part_far(0)
    sum_corner_up(2)
    sum_far(0)
    sum_side(1)
    sum_far(1)
    keys_b(3)
    residual(3)
    part_side(0)
    part_far(2)
    sum_far(2)
    sum_cross(3)
    part_own(3)
    sum_corner_down(3)
    settle_gather()
    part_far(3)
    mean_e()
    sum_corner_up(3)
    part_own(2)
    part_side(3)
    sum_side(0)
    sum_up_far(2)
    sum_down(3)
    sum_up_far(0)
    sum_down_far(1)
    sum_far(3)
    sum_up(3)
    part_side(2)
    sum_up_far(1)
    sum_side(2)
    sum_side(3)
    part_own(1)
    sum_down_far(0)
    mean_f()
    sum_down_far(2)
    sum_down_far(3)
    sum_up_far(3)
    finish(1)
    settle(1)
    finish(0)
    settle(0)
    finish(2)
    settle(2)
    mean_end()
    finish(3)
    for copy in l_later:
        copy.wait()
    for tag in list(sends):
        settle(tag)


def sync(activations, targets, token_ids, sync_fragment, params, adam_m, adam_v, anchor, momentum):
    tokens, width = activations.shape[1:]
    rows, kv = params.shape[1:]
    nq = kv // HEAD
    edge = EDGE * rows // 512
    piece = pltpu.VMEM((nq, rows, HEAD), BF16)
    part = pltpu.VMEM((nq, rows // 2, HEAD), BF16)
    thin = pltpu.VMEM((nq, edge, HEAD), BF16)
    quarter = pltpu.VMEM((rows // 4, HEAD), F32)
    full = jax.ShapeDtypeStruct((rows, kv), F32)
    hbm = pl.BlockSpec(memory_space=pltpu.HBM)
    vmem = pl.BlockSpec(memory_space=pltpu.VMEM)
    return pl.pallas_call(
        functools.partial(sync_kernel, float(width) ** (-0.5)),
        out_shape=(full, jax.ShapeDtypeStruct((4, rows // 4, HEAD), F32)) + (full,) * 5,
        in_specs=[hbm] * 9,
        out_specs=(vmem,) * 7,
        scratch_shapes=[
            pltpu.SMEM(sync_fragment.shape, jnp.int32),
            pltpu.VMEM((2 * tokens, width // 2), BF16),
            pltpu.VMEM((NF // 2, rows, 2 * tokens), BF16),
            pltpu.VMEM((tokens, kv), BF16),
            pltpu.VMEM((1, tokens), jnp.int32),
            pltpu.VMEM((tokens, HEAD), F32),
            pltpu.VMEM((8, HEAD), F32),
            pltpu.VMEM((nq, NF // 2, rows, HEAD), BF16),
            pltpu.VMEM((nq, 2 * tokens, HEAD), F32),
            pltpu.VMEM((nq, tokens, HEAD), F32),
            pltpu.VMEM((nq, tokens, HEAD), F32),
            pltpu.VMEM((nq, 2 * tokens, HEAD), BF16),
            pltpu.VMEM((nq, 5, rows, HEAD), F32),
            piece, piece, piece, thin, thin, part, part, piece, piece, piece,
            piece, piece, piece, part, part, piece, piece, piece,
            pltpu.VMEM((4, rows // 4, HEAD), F32),
            pltpu.VMEM((2, rows // 4, HEAD), F32), quarter, quarter,
            pltpu.VMEM((2, rows // 4, HEAD), F32), quarter, quarter, quarter,
            pltpu.VMEM((4, 8, HEAD), F32),
            pltpu.VMEM((4, 8, HEAD), F32),
            pltpu.SemaphoreType.DMA((nq, KINDS)),
            pltpu.SemaphoreType.DMA((nq, KINDS)),
            pltpu.SemaphoreType.DMA((6,)),
            pltpu.SemaphoreType.DMA((6,)),
            pltpu.SemaphoreType.DMA((4,)),
            pltpu.SemaphoreType.DMA((4,)),
            pltpu.SemaphoreType.DMA((NF // 2,)),
            pltpu.SemaphoreType.DMA((NF // 2,)),
            pltpu.SemaphoreType.DMA((nq + 8 + NF // 2,)),
        ],
        compiler_params=pltpu.CompilerParams(
            collective_id=0, has_side_effects=True, vmem_limit_bytes=36 * 2**20
        ),
        cost_estimate=pl.CostEstimate(
            flops=4 * tokens * width * kv, bytes_accessed=2 * tokens * width + 12 * rows * kv, transcendentals=0
        ),
        name="sync",
    )(*[
        pltpu.with_memory_space_constraint(a, pltpu.HBM)
        for a in (activations, targets, token_ids, sync_fragment, params, adam_m, adam_v, anchor, momentum)
    ])


def update_kernel(steps, frag, grad, delta, params, adam_m, adam_v, anchor, momentum,
                  out_params, out_m, out_v, out_anchor, out_momentum,
                  new_params, new_m, new_v, new_anchor, new_momentum, sem):
    rows = grad.shape[0]
    size = rows // steps
    copies = []

    def store(src, dst):
        copy = pltpu.make_async_copy(src, dst, sem.at[len(copies)])
        copy.start()
        copies.append(copy)

    fragment = pl.ds(pl.multiple_of(frag[0] * HEAD, HEAD), HEAD)
    arriving = pl.ds(pl.multiple_of(frag[1] * HEAD, HEAD), HEAD)
    for i in range(steps):
        r = pl.ds(i * size, size)
        slope = grad[r]
        weight = params[r]
        first = beta_one * adam_m[r] + (1.0 - beta_one) * slope
        second = beta_two * adam_v[r] + (1.0 - beta_two) * slope * slope
        new_m[r] = first
        store(new_m.at[r], out_m.at[0, r])
        new_v[r] = second
        store(new_v.at[r], out_v.at[0, r])
        new_params[r] = weight - learn_rate * (first / (jnp.sqrt(second) + adam_epsilon) + decay_rate * weight)
        new_params[r, arriving] = merge_weight * new_params[r, arriving] + (1.0 - merge_weight) * anchor[r, arriving]
        store(new_params.at[r], out_params.at[0, r])
        new_anchor[r] = anchor[r]
        new_momentum[r] = momentum[r]
        change = delta[r]
        moment = outer_beta * momentum[r, fragment] + change
        new_momentum[r, fragment] = moment
        store(new_momentum.at[r], out_momentum.at[r])
        new_anchor[r, fragment] = anchor[r, fragment] - outer_rate * (change + outer_beta * moment)
        store(new_anchor.at[r], out_anchor.at[r])
    for copy in copies:
        copy.wait()


def update(frag, grad, delta, params, adam_m, adam_v, anchor, momentum, steps=4):
    rows, kv = grad.shape
    vmem = pl.BlockSpec(memory_space=pltpu.VMEM)
    hbm = pl.BlockSpec(memory_space=pltpu.HBM)
    return pl.pallas_call(
        functools.partial(update_kernel, steps),
        out_shape=[jax.ShapeDtypeStruct((1, rows, kv), F32)] * 3 + [jax.ShapeDtypeStruct((rows, kv), F32)] * 2,
        in_specs=[pl.BlockSpec(memory_space=pltpu.SMEM)] + [vmem] * 7,
        out_specs=[hbm] * 5,
        scratch_shapes=[pltpu.VMEM((rows, kv), F32)] * 5 + [pltpu.SemaphoreType.DMA((5 * steps,))],
        compiler_params=pltpu.CompilerParams(vmem_limit_bytes=16 * 2**20),
        name="update",
    )(frag, grad, delta, params, adam_m, adam_v, anchor, momentum)


def on_device(activations, targets, token_ids, sync_fragment, params, adam_m, adam_v, anchor, momentum):
    grad, delta, *held = sync(activations, targets, token_ids, sync_fragment, params, adam_m, adam_v, anchor, momentum)
    delta = delta.reshape(delta.shape[0] * delta.shape[1], delta.shape[2])
    return tuple(update(sync_fragment, grad, delta, *held))


def solution(mesh):
    worker = P("group", "fsdp", None)
    shared = P("fsdp", None)
    return jax.shard_map(
        on_device,
        mesh=mesh,
        in_specs=(worker, worker, P("group", "fsdp"), P(), worker, worker, worker, shared, shared),
        out_specs=(worker, worker, worker, shared, shared),
        check_vma=False,
    )
```

time: 73 us -> 71.3 us (0.977)
  the two profiles are of different devices: /device:TPU:1 before, /device:TPU:160 now
where the time goes in v3:
time: 71.3 us; the launch traced here: 70.7 us
  Pallas kernels  69.9 us (98%)
  between operations  0.82 us (1%)
    pallas_call x1, Pallas kernels, sync(): pl.pallas_call(functools.partial(sync_kernel, float(width) ** (-0.5)), ou...  66.7 us
    pallas_call x1, Pallas kernels, update(): pl.pallas_call(functools.partial(update_kernel, steps), out_shape=[jax.Sh...  3.17 us

profile of v3, /device:TPU:160, one launch (start us, length us, event | category | flops | bytes accessed | tf_op | source)
XLA Modules:
  0.0 70.7 jit_solution(5691798835903596311)
XLA Ops:
  0.6 0.0 copy-start
  0.6 66.7 %sync.1 = (f32[512,512]{1,0:T(8,128)S(1)}, f32[4,128,128]{2,1,0:T(8,128)S(1)}, f32[512,512]{1,0:T(8,128)S(1)}, f32[512,512]{1,0:T(8,128)S(1)}, f32[512,512]{1,0:...) custom-call(bf16[1,256,8192]{2,1,0:T(8,128)(2,1)} %act.1, bf16[1,256,512]{2,1,0:T(8,128)(2,1)} %tgt.1, ...), custom_call_target="tpu_custom_call" | custom-call | flops 4294967296 | bytes 7340032 | tf_op jit(solution)/shard_map/sync/pallas_call | solution.py:517
  67.4 0.0 copy-done
  67.4 3.2 %update.1 = (f32[1,512,512]{2,1,0:T(8,128)}, f32[1,512,512]{2,1,0:T(8,128)}, f32[1,512,512]{2,1,0:T(8,128)}, f32[512,512]{1,0:T(8,128)}, f32[512,512]{1,0:T(8,128)}) custom-call(s32[4]{0:T(128)S(1)} %copy-done, f32[512,512]{1,0:T(8,128)S(1)} %get-tuple-element.12.grad, f32[512,128]{1,0:T(8,128)S(1)} %bitcast.1, f32[512,512]{1,0:T(8,128)S(1)} %get-tuple-element.14.params, ...), custom_call_target="tpu_custom_call" | custom-call | tf_op jit(solution)/shard_map/update/pallas_call | solution.py:609
Async XLA Ops:
  0.6 66.7 %copy-start = (s32[4]{0:T(128)S(1)}, s32[4]{0:T(128)}, u32[]{:S(2)}) copy-start(s32[4]{0:T(128)} %frag.1) | copy-start | bytes 52

commit v4 on v3

--- a/solution.py
+++ b/solution.py
@@ -36,7 +36,7 @@
                 frag, xk, xt, tv, iv, live, total, wg, acc, ksend, krecv, rs, gown,
                 rx1, ry1p, ry1m, rxep, rxem, ry2p, ry2m, ry3p, ry3m, rx2,
                 tx1, ty1p, ty1m, ty2p, ty2m, ty3p, ty3m, tx2,
-                dd, sum_b, sum_c, sum_d, from_b, from_c, from_d, from_e, cs, cr,
+                dd, sum_b, sum_c, from_b, from_c, from_d, from_upper, cs, cr,
                 ssem, rsem, zsem, zrsem, csem, crsem, xsem, xrsem, lsem):
     nq, _, rows, cw = wg.shape
     tokens = iv.shape[1]
@@ -56,11 +56,19 @@
 
     sib, up, down, side = ((g, at(y, x, co)), (g, at(yp, x, c)), (g, at(ym, x, c)), (g, at(y, xo, c)))
 
-    b0, b1, b2 = lax.rem(z, 2), lax.rem(z // 2, 2), z // 4
-    flip0, flip1, flip2, across = ((g + 1 - 2 * b0, me), (g + 2 - 4 * b1, me), (g + 4 - 8 * b2, me), (g + 8 - 16 * far, me))
-    partners = [flip0, flip1, flip2, across] if groups > 1 else []
-    odd = lax.rem(b0 + b1 + far, 2)
-    lower = (1 - b2) * (b0 + b1 + far) + b2 * (1 + 3 * odd)
+    b0, b1, upper = lax.rem(z, 2), lax.rem(z // 2, 2), z // 4
+    mine, other = 2 * b0 + b1, 2 * b0 + 1 - b1
+    flip0, flip1, across = (g + 1 - 2 * b0, me), (g + 2 - 4 * b1, me), (g + 8 - 16 * far, me)
+    before = b0 + b1 + far
+
+    def holder(k):
+        return (far * NZ + k // 2 + 2 * (k % 2), me)
+
+    def hearer(k):
+        return (far * NZ + 4 + k // 2 + 2 * (k % 2), me)
+
+    grouped = groups > 1
+    is_lower, is_upper = upper == 0, upper == 1
 
     neighbours = [sib, up, down, side]
     barrier = pltpu.get_barrier_semaphore()
@@ -147,6 +155,16 @@
             src_ref=src, dst_ref=dst, send_sem=zsem.at[k], recv_sem=zrsem.at[k],
             device_id=peer, device_id_type=MESH)
 
+    def to_holder(k):
+        return pltpu.make_async_remote_copy(
+            src_ref=dd.at[k], dst_ref=from_upper.at[mine], send_sem=zsem.at[6 + k], recv_sem=zrsem.at[6 + mine],
+            device_id=holder(k), device_id_type=MESH)
+
+    def to_hearer(k):
+        return pltpu.make_async_remote_copy(
+            src_ref=delta_out.at[mine], dst_ref=delta_out.at[mine], send_sem=zsem.at[10 + k], recv_sem=zrsem.at[10 + mine],
+            device_id=hearer(k), device_id_type=MESH)
+
     def mean_start():
         l_anchor.wait()
         l_frag.wait()
@@ -154,49 +172,77 @@
         for f in range(1, nq):
             diff = jnp.where(jnp.full(diff.shape, frag[0]) == f, av[:, columns(f)] - pv[:, columns(f)], diff)
         dd[...] = diff.reshape(dd.shape)
-        if groups > 1:
-            @pl.when(lower < 4)
-            def _():
-                pl.semaphore_wait(barrier, 4 - lower)
-
-            start(zcopy(dd.at[pl.ds(2 - 2 * b0, 2)], from_b, 0, flip0))
+        if grouped:
+            @pl.when(is_upper)
+            def _():
+                for k in range(4):
+                    to_holder(k).start()
+
+    def mean_a():
+        if grouped:
+            @pl.when(is_lower)
+            def _():
+                pl.semaphore_wait(barrier, 7 - before)
+                zcopy(dd.at[pl.ds(2 - 2 * b0, 2)], from_b, 0, flip0).start()
 
     def mean_b():
-        if groups > 1:
-            zcopy(from_b, from_b, 0, flip0).wait_recv()
-            sum_b[...] = dd[pl.ds(2 * b0, 2)] + from_b[...]
-            start(zcopy(sum_b.at[1 - b1], from_c, 1, flip1))
+        if grouped:
+            @pl.when(is_lower)
+            def _():
+                zcopy(from_b, from_b, 0, flip0).wait_recv()
+                sum_b[...] = dd[pl.ds(2 * b0, 2)] + from_b[...]
+                zcopy(sum_b.at[1 - b1], from_c, 1, flip1).start()
 
     def mean_c():
-        if groups > 1:
-            zcopy(from_c, from_c, 1, flip1).wait_recv()
-            sum_c[...] = sum_b[b1] + from_c[...]
-            start(zcopy(sum_c, from_d, 2, across))
+        if grouped:
+            @pl.when(is_lower)
+            def _():
+                zcopy(from_c, from_c, 1, flip1).wait_recv()
+                s = sum_b[b1] + from_c[...]
+                for k in range(4):
+                    slot = from_upper.at[k]
+                    zcopy(slot, slot, 6 + k, flip1).wait_recv()
+                    s = s + from_upper[k]
+                sum_c[...] = s
+                zcopy(sum_c, from_d, 2, across).start()
 
     def mean_d():
-        if groups > 1:
-            zcopy(from_d, from_d, 2, across).wait_recv()
-            sum_d[...] = sum_c[...] + from_d[...]
-            start(zcopy(sum_d, from_e, 3, flip2))
-
-    mine, other = 2 * b0 + b1, 2 * b0 + 1 - b1
+        if grouped:
+            @pl.when(is_lower)
+            def _():
+                zcopy(from_d, from_d, 2, across).wait_recv()
+                delta_out[mine] = (sum_c[...] + from_d[...]) / groups
+                zcopy(delta_out.at[mine], delta_out.at[mine], 4, flip1).start()
+                for k in range(4):
+                    to_hearer(k).start()
 
     def mean_e():
-        if groups > 1:
-            zcopy(from_e, from_e, 3, flip2).wait_recv()
-            delta_out[mine] = (sum_d[...] + from_e[...]) / groups
-            start(zcopy(delta_out.at[mine], delta_out.at[mine], 4, flip1))
-
-    def mean_f():
-        if groups > 1:
-            zcopy(delta_out.at[other], delta_out.at[other], 4, flip1).wait_recv()
-            half_done = delta_out.at[pl.ds(2 * b0, 2)]
-            start(zcopy(half_done, half_done, 5, flip0))
+        if grouped:
+            @pl.when(is_lower)
+            def _():
+                zcopy(delta_out.at[other], delta_out.at[other], 4, flip1).wait_recv()
+                half_done = delta_out.at[pl.ds(2 * b0, 2)]
+                zcopy(half_done, half_done, 5, flip0).start()
 
     def mean_end():
-        if groups > 1:
-            half_done = delta_out.at[pl.ds(2 - 2 * b0, 2)]
-            zcopy(half_done, half_done, 5, flip0).wait_recv()
+        if grouped:
+            @pl.when(is_lower)
+            def _():
+                half_done = delta_out.at[pl.ds(2 - 2 * b0, 2)]
+                zcopy(half_done, half_done, 5, flip0).wait_recv()
+                for copy in (zcopy(from_b, from_b, 0, flip0), zcopy(from_c, from_c, 1, flip1), zcopy(sum_c, from_d, 2, across),
+                             zcopy(sum_c, from_d, 4, flip1), zcopy(half_done, half_done, 5, flip0)):
+                    copy.wait_send()
+                for k in range(4):
+                    to_hearer(k).wait_send()
+
+            @pl.when(is_upper)
+            def _():
+                for k in range(4):
+                    slot = delta_out.at[k]
+                    zcopy(slot, slot, 10 + k, flip1).wait_recv()
+                for k in range(4):
+                    to_holder(k).wait_send()
         else:
             delta_out[...] = dd[...]
 
@@ -379,123 +425,133 @@
         grad_out[:, columns(q)] = s * scale
 
     cast(0)
-    pl.semaphore_wait(barrier, len(neighbours) + (lower if groups > 1 else 0))
-    greet(partners)
+    if grouped:
+        pl.semaphore_wait(barrier, len(neighbours) + (1 - upper) * before + upper * 4)
+
+        @pl.when(is_lower)
+        def _():
+            greet([flip0, flip1, across] + [hearer(k) for k in range(4)])
+
+        @pl.when(is_upper)
+        def _():
+            greet([holder(k) for k in range(4)])
+    else:
+        pl.semaphore_wait(barrier, len(neighbours))
     own(0)
+    swap_start()
+    own(2)
     own(1)
+    own(3)
+    mean_start()
+    swap_end()
     count(0)
     count(1)
-    own(2)
-    swap_start()
-    swap_end()
+    turn(7)
+    from_up(0)
+    turn(2)
+    turn(1)
+    mean_a()
+    from_down(0)
     from_up(1)
+    turn(3)
+    turn(5)
+    from_down(1)
+    turn(0)
+    from_up(2)
+    turn(6)
+    turn(4)
     count(2)
-    turn(5)
-    from_down(0)
-    from_up(0)
-    own(3)
-    turn(4)
-    mean_start()
+    from_down(3)
+    from_side(0)
     far_lo(0)
-    from_up(2)
-    from_down(1)
-    turn(2)
+    from_side(1)
     far_hi(0)
-    from_down(2)
+    mean_b()
+    keys_a(0)
+    far_lo(1)
     far_hi(1)
     count(3)
-    from_side(0)
-    from_side(1)
-    from_down(3)
+    from_up(3)
+    from_down(2)
+    keys_a(1)
+    far_hi(2)
     from_side(2)
-    mean_b()
     keys_a(2)
-    far_lo(1)
-    keys_a(0)
-    turn(6)
-    from_up(3)
-    keys_a(1)
-    turn(0)
+    keys_b(0)
+    from_side(3)
+    mean_c()
+    keys_b(1)
+    far_lo(3)
     count(4)
-    far_hi(2)
-    far_lo(2)
-    turn(3)
-    from_side(3)
-    turn(7)
-    turn(1)
-    keys_b(0)
     l_tgt.wait()
     residual(0)
-    mean_c()
-    keys_b(1)
+    far_lo(2)
+    keys_a(3)
+    far_hi(3)
+    residual(1)
     sum_cross(0)
     sum_corner_up(0)
-    residual(1)
-    far_hi(3)
     sum_corner_down(0)
     sum_up(0)
-    far_lo(3)
-    part_own(0)
-    sum_down(1)
-    keys_b(2)
-    mean_d()
     sum_corner_up(1)
     sum_down(0)
+    keys_b(2)
+    sum_corner_down(1)
+    keys_b(3)
+    sum_cross(1)
     residual(2)
-    sum_cross(1)
-    sum_corner_down(1)
-    keys_a(3)
+    part_far(0)
+    sum_far(0)
+    mean_d()
+    residual(3)
+    sum_corner_up(2)
     sum_corner_down(2)
-    sum_down(2)
-    sum_up(1)
     sum_cross(2)
     part_far(1)
-    sum_up(2)
-    part_side(1)
-    part_far(0)
-    sum_corner_up(2)
-    sum_far(0)
-    sum_side(1)
-    sum_far(1)
-    keys_b(3)
-    residual(3)
-    part_side(0)
-    part_far(2)
-    sum_far(2)
-    sum_cross(3)
-    part_own(3)
     sum_corner_down(3)
     settle_gather()
+    sum_corner_up(3)
+    sum_down_far(0)
+    sum_down(2)
+    sum_cross(3)
+    sum_up_far(0)
+    part_side(1)
+    part_side(0)
+    sum_far(1)
+    part_far(2)
+    sum_down(1)
+    part_side(3)
     part_far(3)
+    part_side(2)
+    sum_side(0)
+    sum_side(1)
+    sum_far(2)
+    sum_side(3)
+    sum_far(3)
+    sum_side(2)
+    sum_up(2)
+    sum_up(3)
+    sum_up(1)
+    sum_up_far(1)
     mean_e()
-    sum_corner_up(3)
+    part_own(1)
+    sum_down(3)
+    sum_down_far(1)
+    part_own(0)
     part_own(2)
-    part_side(3)
-    sum_side(0)
-    sum_up_far(2)
-    sum_down(3)
-    sum_up_far(0)
-    sum_down_far(1)
-    sum_far(3)
-    sum_up(3)
-    part_side(2)
-    sum_up_far(1)
-    sum_side(2)
-    sum_side(3)
-    part_own(1)
-    sum_down_far(0)
-    mean_f()
-    sum_down_far(2)
     sum_down_far(3)
     sum_up_far(3)
+    part_own(3)
+    sum_down_far(2)
+    sum_up_far(2)
+    finish(0)
+    settle(0)
     finish(1)
     settle(1)
-    finish(0)
-    settle(0)
+    finish(3)
+    settle(3)
+    mean_end()
     finish(2)
-    settle(2)
-    mean_end()
-    finish(3)
     for copy in l_later:
         copy.wait()
     for tag in list(sends):
@@ -536,14 +592,15 @@
             piece, piece, piece, thin, thin, part, part, piece, piece, piece,
             piece, piece, piece, part, part, piece, piece, piece,
             pltpu.VMEM((4, rows // 4, HEAD), F32),
+            pltpu.VMEM((2, rows // 4, HEAD), F32), quarter,
             pltpu.VMEM((2, rows // 4, HEAD), F32), quarter, quarter,
-            pltpu.VMEM((2, rows // 4, HEAD), F32), quarter, quarter, quarter,
+            pltpu.VMEM((4, rows // 4, HEAD), F32),
             pltpu.VMEM((4, 8, HEAD), F32),
             pltpu.VMEM((4, 8, HEAD), F32),
             pltpu.SemaphoreType.DMA((nq, KINDS)),
             pltpu.SemaphoreType.DMA((nq, KINDS)),
-            pltpu.SemaphoreType.DMA((6,)),
-            pltpu.SemaphoreType.DMA((6,)),
+            pltpu.SemaphoreType.DMA((14,)),
+            pltpu.SemaphoreType.DMA((14,)),
             pltpu.SemaphoreType.DMA((4,)),
             pltpu.SemaphoreType.DMA((4,)),
             pltpu.SemaphoreType.DMA((NF // 2,)),

time: 71.3 us -> 69.4 us (0.973)
  the two profiles are of different devices: /device:TPU:160 before, /device:TPU:228 now
where the time goes in v4:
time: 69.4 us; the launch traced here: 69.3 us
  Pallas kernels  68.5 us (99%)
  between operations  0.82 us (1%)
    pallas_call x1, Pallas kernels, sync(): pl.pallas_call(functools.partial(sync_kernel, float(width) ** (-0.5)), ou...  65.3 us
    pallas_call x1, Pallas kernels, update(): pl.pallas_call(functools.partial(update_kernel, steps), out_shape=[jax.Sh...  3.17 us

profile of v4, /device:TPU:228, one launch (start us, length us, event | category | flops | bytes accessed | tf_op | source)
XLA Modules:
  0.0 69.3 jit_solution(8414037970890907636)
XLA Ops:
  0.6 0.0 copy-start
  0.6 65.3 %sync.1 = (f32[512,512]{1,0:T(8,128)S(1)}, f32[4,128,128]{2,1,0:T(8,128)S(1)}, f32[512,512]{1,0:T(8,128)S(1)}, f32[512,512]{1,0:T(8,128)S(1)}, f32[512,512]{1,0:...) custom-call(bf16[1,256,8192]{2,1,0:T(8,128)(2,1)} %act.1, bf16[1,256,512]{2,1,0:T(8,128)(2,1)} %tgt.1, ...), custom_call_target="tpu_custom_call" | custom-call | flops 4294967296 | bytes 7340032 | tf_op jit(solution)/shard_map/sync/pallas_call | solution.py:573
  66.0 0.0 copy-done
  66.0 3.2 %update.1 = (f32[1,512,512]{2,1,0:T(8,128)}, f32[1,512,512]{2,1,0:T(8,128)}, f32[1,512,512]{2,1,0:T(8,128)}, f32[512,512]{1,0:T(8,128)}, f32[512,512]{1,0:T(8,128)}) custom-call(s32[4]{0:T(128)S(1)} %copy-done, f32[512,512]{1,0:T(8,128)S(1)} %get-tuple-element.12.grad, f32[512,128]{1,0:T(8,128)S(1)} %bitcast.1, f32[512,512]{1,0:T(8,128)S(1)} %get-tuple-element.14.params, ...), custom_call_target="tpu_custom_call" | custom-call | tf_op jit(solution)/shard_map/update/pallas_call | solution.py:666
Async XLA Ops:
  0.6 65.4 %copy-start = (s32[4]{0:T(128)S(1)}, s32[4]{0:T(128)}, u32[]{:S(2)}) copy-start(s32[4]{0:T(128)} %frag.1) | copy-start | bytes 52

commit v5 on v4

--- a/solution.py
+++ b/solution.py
@@ -36,7 +36,7 @@
                 frag, xk, xt, tv, iv, live, total, wg, acc, ksend, krecv, rs, gown,
                 rx1, ry1p, ry1m, rxep, rxem, ry2p, ry2m, ry3p, ry3m, rx2,
                 tx1, ty1p, ty1m, ty2p, ty2m, ty3p, ty3m, tx2,
-                dd, sum_b, sum_c, from_b, from_c, from_d, from_upper, cs, cr,
+                dd, sum_b, sum_c, from_b, from_c, from_near, from_far, total_c, from_upper, cs, cr,
                 ssem, rsem, zsem, zrsem, csem, crsem, xsem, xrsem, lsem):
     nq, _, rows, cw = wg.shape
     tokens = iv.shape[1]
@@ -58,17 +58,17 @@
 
     b0, b1, upper = lax.rem(z, 2), lax.rem(z // 2, 2), z // 4
     mine, other = 2 * b0 + b1, 2 * b0 + 1 - b1
-    flip0, flip1, across = (g + 1 - 2 * b0, me), (g + 2 - 4 * b1, me), (g + 8 - 16 * far, me)
-    before = b0 + b1 + far
-
-    def holder(k):
-        return (far * NZ + k // 2 + 2 * (k % 2), me)
-
-    def hearer(k):
-        return (far * NZ + 4 + k // 2 + 2 * (k % 2), me)
+    flip0, flip1 = (g + 1 - 2 * b0, me), (g + 2 - 4 * b1, me)
+    facing = (1 - upper) * 4 + 2 * (1 - b1)
+    mate, opposite = (far * NZ + facing + b0, me), ((1 - far) * NZ + facing + b0, me)
+    before = b0 + b1
+
+    def faced(k):
+        return (far * NZ + facing + k, me)
 
     grouped = groups > 1
     is_lower, is_upper = upper == 0, upper == 1
+    adds = upper * far == 1
 
     neighbours = [sib, up, down, side]
     barrier = pltpu.get_barrier_semaphore()
@@ -157,13 +157,13 @@
 
     def to_holder(k):
         return pltpu.make_async_remote_copy(
-            src_ref=dd.at[k], dst_ref=from_upper.at[mine], send_sem=zsem.at[6 + k], recv_sem=zrsem.at[6 + mine],
-            device_id=holder(k), device_id_type=MESH)
-
-    def to_hearer(k):
+            src_ref=dd.at[pl.ds(2 * k, 2)], dst_ref=from_upper.at[b0], send_sem=zsem.at[6 + k], recv_sem=zrsem.at[6 + b0],
+            device_id=faced(k), device_id_type=MESH)
+
+    def to_hearer(k, quarter, i):
         return pltpu.make_async_remote_copy(
-            src_ref=delta_out.at[mine], dst_ref=delta_out.at[mine], send_sem=zsem.at[10 + k], recv_sem=zrsem.at[10 + mine],
-            device_id=hearer(k), device_id_type=MESH)
+            src_ref=delta_out.at[quarter], dst_ref=delta_out.at[quarter], send_sem=zsem.at[8 + i], recv_sem=zrsem.at[10 + quarter],
+            device_id=faced(k), device_id_type=MESH)
 
     def mean_start():
         l_anchor.wait()
@@ -175,14 +175,14 @@
         if grouped:
             @pl.when(is_upper)
             def _():
-                for k in range(4):
+                for k in range(2):
                     to_holder(k).start()
 
     def mean_a():
         if grouped:
             @pl.when(is_lower)
             def _():
-                pl.semaphore_wait(barrier, 7 - before)
+                pl.semaphore_wait(barrier, 5 - before - far)
                 zcopy(dd.at[pl.ds(2 - 2 * b0, 2)], from_b, 0, flip0).start()
 
     def mean_b():
@@ -190,7 +190,11 @@
             @pl.when(is_lower)
             def _():
                 zcopy(from_b, from_b, 0, flip0).wait_recv()
-                sum_b[...] = dd[pl.ds(2 * b0, 2)] + from_b[...]
+                s = dd[pl.ds(2 * b0, 2)] + from_b[...]
+                for k in range(2):
+                    zcopy(from_upper.at[k], from_upper.at[k], 6 + k, flip0).wait_recv()
+                    s = s + from_upper[k]
+                sum_b[...] = s
                 zcopy(sum_b.at[1 - b1], from_c, 1, flip1).start()
 
     def mean_c():
@@ -198,31 +202,39 @@
             @pl.when(is_lower)
             def _():
                 zcopy(from_c, from_c, 1, flip1).wait_recv()
-                s = sum_b[b1] + from_c[...]
-                for k in range(4):
-                    slot = from_upper.at[k]
-                    zcopy(slot, slot, 6 + k, flip1).wait_recv()
-                    s = s + from_upper[k]
-                sum_c[...] = s
-                zcopy(sum_c, from_d, 2, across).start()
+                sum_c[...] = sum_b[b1] + from_c[...]
+                pl.when(far == 1)(lambda: zcopy(sum_c, from_near, 2, mate).start())
+                pl.when(far == 0)(lambda: zcopy(sum_c, from_far, 3, opposite).start())
 
     def mean_d():
         if grouped:
-            @pl.when(is_lower)
-            def _():
-                zcopy(from_d, from_d, 2, across).wait_recv()
-                delta_out[mine] = (sum_c[...] + from_d[...]) / groups
-                zcopy(delta_out.at[mine], delta_out.at[mine], 4, flip1).start()
-                for k in range(4):
-                    to_hearer(k).start()
+            @pl.when(adds)
+            def _():
+                zcopy(from_near, from_near, 2, mate).wait_recv()
+                zcopy(from_far, from_far, 3, opposite).wait_recv()
+                total_c[...] = (from_near[...] + from_far[...]) / groups
+                zcopy(total_c, delta_out.at[other], 14, mate).start()
+                zcopy(total_c, delta_out.at[other], 15, opposite).start()
 
     def mean_e():
         if grouped:
             @pl.when(is_lower)
             def _():
+                pl.when(far == 1)(lambda: zcopy(delta_out.at[mine], delta_out.at[mine], 14, mate).wait_recv())
+                pl.when(far == 0)(lambda: zcopy(delta_out.at[mine], delta_out.at[mine], 15, opposite).wait_recv())
+                zcopy(delta_out.at[mine], delta_out.at[mine], 4, flip1).start()
+                to_hearer(0, mine, 0).start()
+                to_hearer(1, mine, 1).start()
+
+    def mean_f():
+        if grouped:
+            @pl.when(is_lower)
+            def _():
                 zcopy(delta_out.at[other], delta_out.at[other], 4, flip1).wait_recv()
                 half_done = delta_out.at[pl.ds(2 * b0, 2)]
                 zcopy(half_done, half_done, 5, flip0).start()
+                to_hearer(0, other, 2).start()
+                to_hearer(1, other, 3).start()
 
     def mean_end():
         if grouped:
@@ -230,19 +242,25 @@
             def _():
                 half_done = delta_out.at[pl.ds(2 - 2 * b0, 2)]
                 zcopy(half_done, half_done, 5, flip0).wait_recv()
-                for copy in (zcopy(from_b, from_b, 0, flip0), zcopy(from_c, from_c, 1, flip1), zcopy(sum_c, from_d, 2, across),
-                             zcopy(sum_c, from_d, 4, flip1), zcopy(half_done, half_done, 5, flip0)):
+                for copy in (zcopy(from_b, from_b, 0, flip0), zcopy(from_c, from_c, 1, flip1),
+                             zcopy(sum_c, from_c, 4, flip1), zcopy(half_done, half_done, 5, flip0)):
                     copy.wait_send()
+                pl.when(far == 1)(lambda: zcopy(sum_c, from_near, 2, mate).wait_send())
+                pl.when(far == 0)(lambda: zcopy(sum_c, from_far, 3, opposite).wait_send())
                 for k in range(4):
-                    to_hearer(k).wait_send()
+                    to_hearer(0, mine, k).wait_send()
 
             @pl.when(is_upper)
             def _():
-                for k in range(4):
-                    slot = delta_out.at[k]
-                    zcopy(slot, slot, 10 + k, flip1).wait_recv()
-                for k in range(4):
+                for i in range(4):
+                    zcopy(delta_out.at[i], delta_out.at[i], 10 + i, flip1).wait_recv()
+                for k in range(2):
                     to_holder(k).wait_send()
+
+            @pl.when(adds)
+            def _():
+                zcopy(total_c, total_c, 14, mate).wait_send()
+                zcopy(total_c, total_c, 15, opposite).wait_send()
         else:
             delta_out[...] = dd[...]
 
@@ -426,132 +444,139 @@
 
     cast(0)
     if grouped:
-        pl.semaphore_wait(barrier, len(neighbours) + (1 - upper) * before + upper * 4)
+        pl.semaphore_wait(barrier, len(neighbours) + (1 - upper) * before + upper * (2 + far))
 
         @pl.when(is_lower)
         def _():
-            greet([flip0, flip1, across] + [hearer(k) for k in range(4)])
+            pl.when(b0 == 0)(lambda: greet([flip0]))
+            pl.when(b1 == 0)(lambda: greet([flip1]))
+            greet([faced(1), faced(0)])
+            pl.when(far == 0)(lambda: greet([opposite]))
+            pl.when(b0 == 1)(lambda: greet([flip0]))
+            pl.when(b1 == 1)(lambda: greet([flip1]))
 
         @pl.when(is_upper)
         def _():
-            greet([holder(k) for k in range(4)])
+            greet([faced(0), faced(1)])
+            pl.when(far == 1)(lambda: greet([opposite]))
     else:
         pl.semaphore_wait(barrier, len(neighbours))
     own(0)
+    count(0)
     swap_start()
     own(2)
+    count(1)
     own(1)
     own(3)
     mean_start()
+    mean_a()
     swap_end()
-    count(0)
-    count(1)
     turn(7)
+    from_down(0)
+    from_down(2)
+    count(2)
+    turn(4)
     from_up(0)
+    turn(1)
+    from_side(0)
+    keys_a(0)
+    turn(5)
     turn(2)
-    turn(1)
-    mean_a()
-    from_down(0)
+    turn(3)
     from_up(1)
-    turn(3)
-    turn(5)
     from_down(1)
-    turn(0)
     from_up(2)
     turn(6)
-    turn(4)
-    count(2)
+    turn(0)
+    far_lo(0)
+    far_hi(0)
+    count(3)
+    far_lo(2)
     from_down(3)
-    from_side(0)
-    far_lo(0)
     from_side(1)
-    far_hi(0)
+    keys_a(1)
+    from_side(2)
+    far_hi(1)
+    keys_b(0)
+    far_lo(1)
+    from_side(3)
+    far_hi(2)
+    count(4)
+    from_up(3)
     mean_b()
-    keys_a(0)
-    far_lo(1)
-    far_hi(1)
-    count(3)
-    from_up(3)
-    from_down(2)
-    keys_a(1)
-    far_hi(2)
-    from_side(2)
-    keys_a(2)
-    keys_b(0)
-    from_side(3)
-    mean_c()
-    keys_b(1)
-    far_lo(3)
-    count(4)
     l_tgt.wait()
     residual(0)
-    far_lo(2)
-    keys_a(3)
-    far_hi(3)
-    residual(1)
+    far_lo(3)
+    keys_a(2)
     sum_cross(0)
-    sum_corner_up(0)
-    sum_corner_down(0)
-    sum_up(0)
-    sum_corner_up(1)
+    keys_b(1)
     sum_down(0)
     keys_b(2)
-    sum_corner_down(1)
-    keys_b(3)
-    sum_cross(1)
-    residual(2)
+    sum_corner_up(0)
+    mean_c()
+    residual(1)
+    sum_corner_down(0)
     part_far(0)
     sum_far(0)
+    far_hi(3)
+    sum_up(0)
     mean_d()
+    residual(2)
+    sum_corner_down(1)
+    sum_corner_up(1)
+    sum_cross(1)
+    keys_a(3)
+    sum_corner_down(2)
+    keys_b(3)
+    sum_up_far(0)
+    sum_cross(2)
+    part_side(2)
+    sum_corner_up(2)
+    sum_down_far(0)
+    part_far(1)
     residual(3)
-    sum_corner_up(2)
-    sum_corner_down(2)
-    sum_cross(2)
-    part_far(1)
+    part_side(1)
+    sum_far(1)
+    sum_side(1)
+    part_far(2)
+    sum_up(1)
+    part_own(0)
+    sum_down(2)
+    sum_far(2)
+    sum_cross(3)
+    part_own(1)
+    sum_side(2)
+    sum_down(1)
+    part_own(3)
+    sum_corner_up(3)
+    mean_e()
     sum_corner_down(3)
     settle_gather()
-    sum_corner_up(3)
-    sum_down_far(0)
-    sum_down(2)
-    sum_cross(3)
-    sum_up_far(0)
-    part_side(1)
-    part_side(0)
-    sum_far(1)
-    part_far(2)
-    sum_down(1)
-    part_side(3)
+    sum_down_far(2)
     part_far(3)
-    part_side(2)
-    sum_side(0)
-    sum_side(1)
-    sum_far(2)
-    sum_side(3)
-    sum_far(3)
-    sum_side(2)
     sum_up(2)
     sum_up(3)
-    sum_up(1)
+    part_side(0)
+    sum_far(3)
+    part_side(3)
+    sum_side(0)
+    sum_down(3)
+    sum_up_far(2)
+    sum_side(3)
+    sum_down_far(1)
+    mean_f()
     sum_up_far(1)
-    mean_e()
-    part_own(1)
-    sum_down(3)
-    sum_down_far(1)
-    part_own(0)
-    part_own(2)
     sum_down_far(3)
     sum_up_far(3)
-    part_own(3)
-    sum_down_far(2)
-    sum_up_far(2)
+    part_own(2)
     finish(0)
     settle(0)
+    finish(2)
+    settle(2)
     finish(1)
     settle(1)
     finish(3)
-    settle(3)
     mean_end()
-    finish(2)
     for copy in l_later:
         copy.wait()
     for tag in list(sends):
@@ -593,14 +618,14 @@
             piece, piece, piece, part, part, piece, piece, piece,
             pltpu.VMEM((4, rows // 4, HEAD), F32),
             pltpu.VMEM((2, rows // 4, HEAD), F32), quarter,
-            pltpu.VMEM((2, rows // 4, HEAD), F32), quarter, quarter,
-            pltpu.VMEM((4, rows // 4, HEAD), F32),
+            pltpu.VMEM((2, rows // 4, HEAD), F32), quarter, quarter, quarter, quarter,
+            pltpu.VMEM((2, 2, rows // 4, HEAD), F32),
             pltpu.VMEM((4, 8, HEAD), F32),
             pltpu.VMEM((4, 8, HEAD), F32),
             pltpu.SemaphoreType.DMA((nq, KINDS)),
             pltpu.SemaphoreType.DMA((nq, KINDS)),
-            pltpu.SemaphoreType.DMA((14,)),
-            pltpu.SemaphoreType.DMA((14,)),
+            pltpu.SemaphoreType.DMA((16,)),
+            pltpu.SemaphoreType.DMA((16,)),
             pltpu.SemaphoreType.DMA((4,)),
             pltpu.SemaphoreType.DMA((4,)),
             pltpu.SemaphoreType.DMA((NF // 2,)),

time: 69.4 us -> 68.2 us (0.983)
  the two profiles are of different devices: /device:TPU:228 before, /device:TPU:160 now
where the time goes in v5:
time: 68.2 us; the launch traced here: 68.1 us
  Pallas kernels  67.3 us (99%)
  between operations  0.82 us (1%)
    pallas_call x1, Pallas kernels, sync(): pl.pallas_call(functools.partial(sync_kernel, float(width) ** (-0.5)), ou...  64.1 us
    pallas_call x1, Pallas kernels, update(): pl.pallas_call(functools.partial(update_kernel, steps), out_shape=[jax.Sh...  3.17 us

profile of v5, /device:TPU:160, one launch (start us, length us, event | category | flops | bytes accessed | tf_op | source)
XLA Modules:
  0.0 68.1 jit_solution(17225858812839874062)
XLA Ops:
  0.6 0.0 copy-start
  0.6 64.1 %sync.1 = (f32[512,512]{1,0:T(8,128)S(1)}, f32[4,128,128]{2,1,0:T(8,128)S(1)}, f32[512,512]{1,0:T(8,128)S(1)}, f32[512,512]{1,0:T(8,128)S(1)}, f32[512,512]{1,0:...) custom-call(bf16[1,256,8192]{2,1,0:T(8,128)(2,1)} %act.1, bf16[1,256,512]{2,1,0:T(8,128)(2,1)} %tgt.1, ...), custom_call_target="tpu_custom_call" | custom-call | flops 4294967296 | bytes 7340032 | tf_op jit(solution)/shard_map/sync/pallas_call | solution.py:598
  64.7 0.0 copy-done
  64.7 3.2 %update.1 = (f32[1,512,512]{2,1,0:T(8,128)}, f32[1,512,512]{2,1,0:T(8,128)}, f32[1,512,512]{2,1,0:T(8,128)}, f32[512,512]{1,0:T(8,128)}, f32[512,512]{1,0:T(8,128)}) custom-call(s32[4]{0:T(128)S(1)} %copy-done, f32[512,512]{1,0:T(8,128)S(1)} %get-tuple-element.12.grad, f32[512,128]{1,0:T(8,128)S(1)} %bitcast.1, f32[512,512]{1,0:T(8,128)S(1)} %get-tuple-element.14.params, ...), custom_call_target="tpu_custom_call" | custom-call | tf_op jit(solution)/shard_map/update/pallas_call | solution.py:691
Async XLA Ops:
  0.6 64.1 %copy-start = (s32[4]{0:T(128)S(1)}, s32[4]{0:T(128)}, u32[]{:S(2)}) copy-start(s32[4]{0:T(128)} %frag.1) | copy-start | bytes 52

commit v6 on v5

--- a/solution.py
+++ b/solution.py
@@ -469,7 +469,6 @@
     own(1)
     own(3)
     mean_start()
-    mean_a()
     swap_end()
     turn(7)
     from_down(0)
@@ -479,6 +478,7 @@
     from_up(0)
     turn(1)
     from_side(0)
+    mean_a()
     keys_a(0)
     turn(5)
     turn(2)

time: 68.2 us -> 68.2 us (level)
  no operation moved by 1% of the time
where the time goes in v6:
time: 68.2 us; the launch traced here: 68.1 us
  Pallas kernels  67.3 us (99%)
  between operations  0.82 us (1%)
    pallas_call x1, Pallas kernels, sync(): pl.pallas_call(functools.partial(sync_kernel, float(width) ** (-0.5)), ou...  64.1 us
    pallas_call x1, Pallas kernels, update(): pl.pallas_call(functools.partial(update_kernel, steps), out_shape=[jax.Sh...  3.17 us

profile of v6, /device:TPU:160, one launch (start us, length us, event | category | flops | bytes accessed | tf_op | source)
XLA Modules:
  0.0 68.1 jit_solution(4887396265318060821)
XLA Ops:
  0.6 0.0 copy-start
  0.6 64.1 %sync.1 = (f32[512,512]{1,0:T(8,128)S(1)}, f32[4,128,128]{2,1,0:T(8,128)S(1)}, f32[512,512]{1,0:T(8,128)S(1)}, f32[512,512]{1,0:T(8,128)S(1)}, f32[512,512]{1,0:...) custom-call(bf16[1,256,8192]{2,1,0:T(8,128)(2,1)} %act.1, bf16[1,256,512]{2,1,0:T(8,128)(2,1)} %tgt.1, ...), custom_call_target="tpu_custom_call" | custom-call | flops 4294967296 | bytes 7340032 | tf_op jit(solution)/shard_map/sync/pallas_call | solution.py:598
  64.7 0.0 copy-done
  64.7 3.2 %update.1 = (f32[1,512,512]{2,1,0:T(8,128)}, f32[1,512,512]{2,1,0:T(8,128)}, f32[1,512,512]{2,1,0:T(8,128)}, f32[512,512]{1,0:T(8,128)}, f32[512,512]{1,0:T(8,128)}) custom-call(s32[4]{0:T(128)S(1)} %copy-done, f32[512,512]{1,0:T(8,128)S(1)} %get-tuple-element.12.grad, f32[512,128]{1,0:T(8,128)S(1)} %bitcast.1, f32[512,512]{1,0:T(8,128)S(1)} %get-tuple-element.14.params, ...), custom_call_target="tpu_custom_call" | custom-call | tf_op jit(solution)/shard_map/update/pallas_call | solution.py:691
Async XLA Ops:
  0.6 64.1 %copy-start = (s32[4]{0:T(128)S(1)}, s32[4]{0:T(128)}, u32[]{:S(2)}) copy-start(s32[4]{0:T(128)} %frag.1) | copy-start | bytes 52
